TPU v7x, 256 devices: a whole 4x4x8 slice. The times are simulated.
256 devices in a mesh: tm: 32 (over z, y), rows: 8 (over x, core).
Axes of the slice: x: 4, y: 4, z: 8, core: 2. Of those that a mesh axis runs over, the one named last changes fastest.
Arguments:
- source: bfloat16 [128, 8, 32, 256], P('tm', 'rows'), may hold values from -6 to 6
- frame_counts: int32 [32], P('tm'), may hold values from 1 to 9, as said below
- tap_frames: int32 [288, 4], P('tm'), may hold values from 0 to 127, as said below
- tap_weights: float32 [288, 4], P('tm'), may hold values from 0.1 to 0.6
- kernel_one: bfloat16 [3, 3, 3, 256, 256], replicated, may hold values from -0.078125 to 0.078125
- bias_one: float32 [256], replicated, may hold values from -3 to 3
- kernel_two: bfloat16 [3, 3, 3, 256, 256], replicated, may hold values from -0.078125 to 0.078125
- bias_two: float32 [256], replicated, may hold values from -3 to 3
- upstream: bfloat16 [288, 8, 32, 256], P('tm', 'rows'), may hold values from -6 to 6
Outputs:
- decoded: bfloat16 [288, 8, 32, 256], P('tm', 'rows')
- source_grad: float32 [128, 8, 32, 256], P('tm', 'rows')
Inputs may be any that keep to these rules, and one draw needn't show every extreme that they name: `frame_counts`: counts of spans 2i and 2i + 1 sum to 10; some span holds exactly 9 frames. `tap_frames`: every tap of a used slot of span d lies in source frames 4 * d - 6 to 4 * d + 9; some span reaches the lower end and some span the upper end. Taps of unused slots are ignored.
All inputs are finite; a program needn't handle non-finite values.
Results may differ from a plain program's by a relative error of at most 0.014.
Values may be sent and summed in bfloat16 or wider, within the bound.
A program may use at most 64 MiB of HBM per device.

v0:
```python
import jax
import jax.numpy as jnp
from jax import lax
from jax.sharding import PartitionSpec as P


def extended_2(cells, sides, width):
    for axis, dim in sides:
        count = lax.axis_size(axis)
        ends = count - 1
        head = lax.slice_in_dim(cells, 0, width, axis=dim)
        tail = lax.slice_in_dim(cells, cells.shape[dim] - width, cells.shape[dim], axis=dim)
        cells = jnp.concatenate(
            [
                lax.ppermute(tail, axis, [(i, (i + 1) % count) for i in range(ends)]),
                cells,
                lax.ppermute(head, axis, [((i + 1) % count, i) for i in range(ends)]),
            ],
            axis=dim,
        )
    return cells


def from_behind(x, axis, by):
    devices = lax.axis_size(axis)
    pairs = [(i, i + by) for i in range(devices) if 0 <= i + by < devices]
    return lax.ppermute(x, axis, pairs)


def convolve(extended, kernel):
    return lax.conv_general_dilated(
        extended[None],
        kernel,
        (1, 1, 1),
        "VALID",
        dimension_numbers=("NDHWC", "DHWIO", "NDHWC"),
        preferred_element_type=jnp.float32,
    )[0]


def surround(slab, filled):
    last_frame = lax.dynamic_slice_in_dim(slab, filled - 1, 1, 0)
    edges = extended_2(jnp.concatenate([slab[:1], last_frame], 0), (("tm", 0),), 1)
    extended = jnp.concatenate([edges[:1], slab, jnp.zeros_like(slab[:1])], 0)
    extended = lax.dynamic_update_slice_in_dim(extended, edges[3:], filled + 1, 0)
    extended = extended_2(extended, (("rows", 1),), 1)
    return jnp.pad(extended, ((0, 0), (0, 0), (1, 1), (0, 0)))


def frame_matrix(tap_frames, tap_weights, lowest, length):
    targets = lowest + jnp.arange(length, dtype=jnp.int32)
    hits = tap_frames[:, :, None] == targets[None, None, :]
    return jnp.sum(jnp.where(hits, tap_weights[:, :, None], 0.0), axis=1)


def forward_block(inputs, kernel, bias, filled, occupied):
    widened = inputs.astype(jnp.float32)
    activated = jax.nn.silu(widened).astype(jnp.bfloat16)
    summed = widened + convolve(surround(activated, filled), kernel) + bias
    return jnp.where(occupied, summed, 0.0).astype(jnp.bfloat16)


def backward_block(gradient, inputs, flipped, filled, occupied):
    widened = inputs.astype(jnp.float32)
    logistic = jax.nn.sigmoid(widened)
    deriv = logistic * (1.0 + widened * (1.0 - logistic))
    summed = gradient.astype(jnp.float32) + deriv * convolve(surround(gradient, filled), flipped)
    return jnp.where(occupied, summed, 0.0)


def body(
    source,
    frame_counts,
    tap_frames,
    tap_weights,
    kernel_one,
    bias_one,
    kernel_two,
    bias_two,
    upstream,
):
    held_frames = source.shape[0]
    capacity = upstream.shape[0]
    filled = frame_counts[0]
    occupied = (jnp.arange(capacity, dtype=jnp.int32) < filled)[:, None, None, None]
    position = lax.axis_index("tm")
    fetched = {}
    for offset in (-2, -1, 1, 2):
        fetched[offset] = from_behind(source, "tm", -offset)
    window = jnp.concatenate([fetched[-2], fetched[-1], source, fetched[1], fetched[2]], 0)
    mixing = frame_matrix(tap_frames, tap_weights, (position - 2) * held_frames, window.shape[0])
    blended_rows = jnp.dot(
        mixing,
        window.reshape(window.shape[0], -1).astype(jnp.float32),
        precision=lax.Precision.HIGHEST,
    )
    blended = jnp.where(occupied, blended_rows.reshape(upstream.shape), 0.0).astype(jnp.bfloat16)
    first_out = forward_block(blended, kernel_one, bias_one, filled, occupied)
    decoded = forward_block(first_out, kernel_two, bias_two, filled, occupied)
    flipped_one = jnp.transpose(jnp.flip(kernel_one, (0, 1, 2)), (0, 1, 2, 4, 3))
    flipped_two = jnp.transpose(jnp.flip(kernel_two, (0, 1, 2)), (0, 1, 2, 4, 3))
    incoming = jnp.where(occupied, upstream, jnp.zeros((), jnp.bfloat16))
    grad_mid = backward_block(incoming, first_out, flipped_two, filled, occupied).astype(
        jnp.bfloat16
    )
    grad_low = backward_block(grad_mid, blended, flipped_one, filled, occupied)
    grad_rows = grad_low.reshape(capacity, -1)
    frame_shape = (held_frames,) + upstream.shape[1:]
    spread = jnp.dot(mixing.T, grad_rows, precision=lax.Precision.HIGHEST)
    spread = spread.reshape((5,) + frame_shape)
    source_grad = spread[2]
    for offset in (-2, -1, 1, 2):
        source_grad = source_grad + from_behind(
            spread[2 + offset].astype(jnp.bfloat16), "tm", offset
        ).astype(jnp.float32)
    return (decoded, source_grad)


def solution(mesh):
    return jax.shard_map(
        body,
        mesh=mesh,
        in_specs=(
            P("tm", "rows", None, None),
            P("tm"),
            P("tm", None),
            P("tm", None),
            P(),
            P(),
            P(),
            P(),
            P("tm", "rows", None, None),
        ),
        out_specs=(P("tm", "rows", None, None), P("tm", "rows", None, None)),
        check_vma=False,
    )
```

profile of v0, /device:TPU:122, one launch (start us, length us, event | category | flops | bytes accessed | tf_op | source)
XLA Modules:
  0.0 144.7 jit_solution(16331781493939400910)
XLA Ops:
  0.6 6.0 %collective-permute-start = (bf16[4,1,32,256]{3,2,1,0:T(8,128)(2,1)}, bf16[4,1,32,256]{3,2,1,0:T(8,128)(2,1)}, u32[]{:S(2)}, u32[]{:S(2)}) collective-permute-start(bf16[4,1,32,256]{3,2,1,0:T(8,128)(2,1)} %param.9), channel_id=1, source_target_pairs={{0,16},{8,24},{16,32},{24,40},{32,48},{40,56},{48,64},{56,72},{64,... | collective-permute-start | bytes 196616 | tf_op jit(solution)/shard_map/ppermute | solution.py:27
  6.6 4.1 %collective-permute-start.1 = (bf16[4,1,32,256]{3,2,1,0:T(8,128)(2,1)}, bf16[4,1,32,256]{3,2,1,0:T(8,128)(2,1)}, u32[]{:S(2)}, u32[]{:S(2)}) collective-permute-start(bf16[4,1,32,256]{3,2,1,0:T(8,128)(2,1)} %param.9), channel_id=1, source_target_pairs={{0,8},{8,16},{16,24},{24,32},{32,40},{40,48},{48,56},{56,64},{64,7... | collective-permute-start | bytes 196616 | tf_op jit(solution)/shard_map/ppermute | solution.py:27
  10.7 1.9 %collective-permute-start.2 = (bf16[4,1,32,256]{3,2,1,0:T(8,128)(2,1)}, bf16[4,1,32,256]{3,2,1,0:T(8,128)(2,1)}, u32[]{:S(2)}, u32[]{:S(2)}) collective-permute-start(bf16[4,1,32,256]{3,2,1,0:T(8,128)(2,1)} %param.9), channel_id=1, source_target_pairs={{8,0},{16,8},{24,16},{32,24},{40,32},{48,40},{56,48},{64,56},{72,6... | collective-permute-start | bytes 196616 | tf_op jit(solution)/shard_map/ppermute | solution.py:27
  12.7 1.9 %collective-permute-start.3 = (bf16[4,1,32,256]{3,2,1,0:T(8,128)(2,1)}, bf16[4,1,32,256]{3,2,1,0:T(8,128)(2,1)}, u32[]{:S(2)}, u32[]{:S(2)}) collective-permute-start(bf16[4,1,32,256]{3,2,1,0:T(8,128)(2,1)} %param.9), channel_id=1, source_target_pairs={{16,0},{24,8},{32,16},{40,24},{48,32},{56,40},{64,48},{72,56},{80,... | collective-permute-start | bytes 196616 | tf_op jit(solution)/shard_map/ppermute | solution.py:27
  17.7 7.2 %collective-permute-start.12 = (bf16[1,1,32,256]{3,0,2,1:T(2,128)(2,1)}, bf16[1,1,32,256]{3,0,2,1:T(2,128)(2,1)}, u32[]{:S(2)}, u32[]{:S(2)}) collective-permute-start(bf16[1,1,32,256]{3,0,2,1:T(2,128)(2,1)} %get-tuple-element.21), channel_id=1, source_target_pairs={{0,8},{8,16},{16,24},{24,32},{32,40},{40,48},{48,56},{56,64},{64,7... | collective-permute-start | bytes 49160 | tf_op jit(solution)/shard_map/ppermute | solution.py:15
  32.1 2.0 %multiply_convert_fusion = (bf16[9,32,256]{2,0,1:T(8,128)(2,1)S(1)}, f32[9,32,256]{2,0,1:T(8,128)}) fusion(bf16[32,256,20]{1,0,2:T(8,128)(2,1)S(1)} %slice_bitcast_fusion.4, f32[9,20]{1,0:T(8,128)S(1)} %select_reduce_fusion, pred[9]{0:T(512)(128)(4,1)} %copy-done.12), kind=kOutput, calls=%fused_computation.77 | convolution fusion | flops 18284544 | bytes 770777 | tf_op jit(solution)/shard_map/dot_general | solution.py:92
  35.5 2.8 %collective-permute-start.4 = (bf16[1,1,32,256]{3,0,2,1:T(2,128)(2,1)}, bf16[1,1,32,256]{3,0,2,1:T(2,128)(2,1)}, u32[]{:S(2)}, u32[]{:S(2)}) collective-permute-start(bf16[1,1,32,256]{3,0,2,1:T(2,128)(2,1)} %get-tuple-element.19), channel_id=1, source_target_pairs={{0,8},{8,16},{16,24},{24,32},{32,40},{40,48},{48,56},{56,64},{64,7... | collective-permute-start | bytes 49160 | tf_op jit(solution)/shard_map/ppermute | solution.py:15
  38.4 3.1 %collective-permute-start.5 = (bf16[1,1,32,256]{3,0,2,1:T(2,128)(2,1)}, bf16[1,1,32,256]{3,0,2,1:T(2,128)(2,1)}, u32[]{:S(2)}, u32[]{:S(2)}) collective-permute-start(bf16[1,1,32,256]{3,0,2,1:T(2,128)(2,1)} %get-tuple-element.18), channel_id=1, source_target_pairs={{8,0},{16,8},{24,16},{32,24},{40,32},{48,40},{56,48},{64,56},{72,6... | collective-permute-start | bytes 49160 | tf_op jit(solution)/shard_map/ppermute | solution.py:17
  41.6 2.1 %maximum_maximum_fusion = (bf16[11,1,32,256]{3,0,2,1:T(8,128)(2,1)}, bf16[11,1,32,256]{3,0,2,1:T(8,128)(2,1)}) fusion(bf16[9,1,32,256]{3,0,2,1:T(8,128)(2,1)} %bitcast.196, bf16[1,1,32,256]{3,0,2,1:T(2,128)(2,1)} %collective-permute-done.4, bf16[11]{0:T(256)(128)(2,1)S(1)} %pad.56.clone, bf16[9,1,32,256]{3,0,2,1:T(8,128)(2,1)} %copy-done.7, ...), kind=kLoop, calls=%fused_computation.87 | loop fusion | flops 991232 | bytes 688150 | tf_op jit(solution)/shard_map/concatenate | solution.py:44
  43.8 4.0 %collective-permute-done.5 = bf16[1,1,32,256]{3,0,2,1:T(2,128)(2,1)} collective-permute-done((bf16[1,1,32,256]{3,0,2,1:T(2,128)(2,1)}, bf16[1,1,32,256]{3,0,2,1:T(2,128)(2,1)}, u32[]{:S(2)}, u32[]{:S(2)}) %collective-permute-start.5) | collective-permute-done | bytes 16416 | tf_op jit(solution)/shard_map/ppermute | solution.py:17
  51.4 3.6 %collective-permute-start.7 = (bf16[11,1,32,256]{3,0,2,1:T(8,128)(2,1)}, bf16[11,1,32,256]{3,0,2,1:T(8,128)(2,1)}, u32[]{:S(2)}, u32[]{:S(2)}) collective-permute-start(bf16[11,1,32,256]{3,0,2,1:T(8,128)(2,1)} %dynamic_update_slice.12), channel_id=1, source_target_pairs={{1,0},{2,1},{3,2},{4,3},{5,4},{6,5},{7,6},{9,8},{10,9},{11,10},{12... | collective-permute-start | bytes 540680 | tf_op jit(solution)/shard_map/ppermute | solution.py:17
  55.1 1.9 %collective-permute-start.13 = (bf16[1,1,32,256]{3,0,2,1:T(2,128)(2,1)}, bf16[1,1,32,256]{3,0,2,1:T(2,128)(2,1)}, u32[]{:S(2)}, u32[]{:S(2)}) collective-permute-start(bf16[1,1,32,256]{3,0,2,1:T(2,128)(2,1)} %get-tuple-element.20), channel_id=1, source_target_pairs={{8,0},{16,8},{24,16},{32,24},{40,32},{48,40},{56,48},{64,56},{72,6... | collective-permute-start | bytes 49160 | tf_op jit(solution)/shard_map/ppermute | solution.py:17
  57.0 7.5 %collective-permute-done.13 = bf16[1,1,32,256]{3,0,2,1:T(2,128)(2,1)} collective-permute-done((bf16[1,1,32,256]{3,0,2,1:T(2,128)(2,1)}, bf16[1,1,32,256]{3,0,2,1:T(2,128)(2,1)}, u32[]{:S(2)}, u32[]{:S(2)}) %collective-permute-start.13) | collective-permute-done | bytes 16416 | tf_op jit(solution)/shard_map/ppermute | solution.py:17
  68.1 3.6 %collective-permute-start.15 = (bf16[11,1,32,256]{3,0,2,1:T(8,128)(2,1)}, bf16[11,1,32,256]{3,0,2,1:T(8,128)(2,1)S(1)}, u32[]{:S(2)}, u32[]{:S(2)}) collective-permute-start(bf16[11,1,32,256]{3,0,2,1:T(8,128)(2,1)} %dynamic_update_slice.14), channel_id=1, source_target_pairs={{1,0},{2,1},{3,2},{4,3},{5,4},{6,5},{7,6},{9,8},{10,9},{11,10},{12... | collective-permute-start | bytes 540680 | tf_op jit(solution)/shard_map/ppermute | solution.py:17
  85.2 3.9 %collective-permute-start.17 = (bf16[1,1,32,256]{3,0,2,1:T(2,128)(2,1)S(1)}, bf16[1,1,32,256]{3,0,2,1:T(2,128)(2,1)}, u32[]{:S(2)}, u32[]{:S(2)}) collective-permute-start(bf16[1,1,32,256]{3,0,2,1:T(2,128)(2,1)S(1)} %get-tuple-element.14), channel_id=1, source_target_pairs={{8,0},{16,8},{24,16},{32,24},{40,32},{48,40},{56,48},{64,56},{72,6... | collective-permute-start | bytes 49160 | tf_op jit(solution)/shard_map/ppermute | solution.py:17
  90.2 4.2 %collective-permute-done.17 = bf16[1,1,32,256]{3,0,2,1:T(2,128)(2,1)} collective-permute-done((bf16[1,1,32,256]{3,0,2,1:T(2,128)(2,1)S(1)}, bf16[1,1,32,256]{3,0,2,1:T(2,128)(2,1)}, u32[]{:S(2)}, u32[]{:S(2)}) %collective-permute-start.17) | collective-permute-done | bytes 16416 | tf_op jit(solution)/shard_map/ppermute | solution.py:17
  96.1 2.4 %collective-permute-start.18 = (bf16[11,1,32,256]{3,0,2,1:T(8,128)(2,1)}, bf16[11,1,32,256]{3,0,2,1:T(8,128)(2,1)}, u32[]{:S(2)}, u32[]{:S(2)}) collective-permute-start(bf16[11,1,32,256]{3,0,2,1:T(8,128)(2,1)} %dynamic_update_slice.15), channel_id=1, source_target_pairs={{0,1},{1,2},{2,3},{3,4},{4,5},{5,6},{6,7},{8,9},{9,10},{10,11},{11... | collective-permute-start | bytes 540680 | tf_op jit(solution)/shard_map/ppermute | solution.py:15
  98.5 3.1 %collective-permute-start.19 = (bf16[11,1,32,256]{3,0,2,1:T(8,128)(2,1)}, bf16[11,1,32,256]{3,0,2,1:T(8,128)(2,1)}, u32[]{:S(2)}, u32[]{:S(2)}) collective-permute-start(bf16[11,1,32,256]{3,0,2,1:T(8,128)(2,1)} %dynamic_update_slice.15), channel_id=1, source_target_pairs={{1,0},{2,1},{3,2},{4,3},{5,4},{6,5},{7,6},{9,8},{10,9},{11,10},{12... | collective-permute-start | bytes 540680 | tf_op jit(solution)/shard_map/ppermute | solution.py:17
  101.7 1.9 %collective-permute-start.9 = (bf16[1,1,32,256]{3,0,2,1:T(2,128)(2,1)}, bf16[1,1,32,256]{3,0,2,1:T(2,128)(2,1)}, u32[]{:S(2)}, u32[]{:S(2)}) collective-permute-start(bf16[1,1,32,256]{3,0,2,1:T(2,128)(2,1)} %get-tuple-element.16), channel_id=1, source_target_pairs={{8,0},{16,8},{24,16},{32,24},{40,32},{48,40},{56,48},{64,56},{72,6... | collective-permute-start | bytes 49160 | tf_op jit(solution)/shard_map/ppermute | solution.py:17
  103.6 7.5 %collective-permute-done.9 = bf16[1,1,32,256]{3,0,2,1:T(2,128)(2,1)} collective-permute-done((bf16[1,1,32,256]{3,0,2,1:T(2,128)(2,1)}, bf16[1,1,32,256]{3,0,2,1:T(2,128)(2,1)}, u32[]{:S(2)}, u32[]{:S(2)}) %collective-permute-start.9) | collective-permute-done | bytes 16416 | tf_op jit(solution)/shard_map/ppermute | solution.py:17
  114.8 3.8 %collective-permute-start.11 = (bf16[11,1,32,256]{3,0,2,1:T(8,128)(2,1)}, bf16[11,1,32,256]{3,0,2,1:T(8,128)(2,1)S(1)}, u32[]{:S(2)}, u32[]{:S(2)}) collective-permute-start(bf16[11,1,32,256]{3,0,2,1:T(8,128)(2,1)} %dynamic_update_slice.13), channel_id=1, source_target_pairs={{1,0},{2,1},{3,2},{4,3},{5,4},{6,5},{7,6},{9,8},{10,9},{11,10},{12... | collective-permute-start | bytes 540680 | tf_op jit(solution)/shard_map/ppermute | solution.py:17
  123.9 1.9 %collective-permute-start.20 = (bf16[4,1,32,256]{3,2,1,0:T(8,128)(2,1)S(1)}, bf16[4,1,32,256]{3,2,1,0:T(8,128)(2,1)S(1)}, u32[]{:S(2)}, u32[]{:S(2)}) collective-permute-start(bf16[4,1,32,256]{3,2,1,0:T(8,128)(2,1)S(1)} %bitcast.201), channel_id=1, source_target_pairs={{16,0},{24,8},{32,16},{40,24},{48,32},{56,40},{64,48},{72,56},{80,... | collective-permute-start | bytes 196616 | tf_op jit(solution)/shard_map/ppermute | solution.py:27
  127.8 7.2 %collective-permute-start.22 = (bf16[4,1,32,256]{3,2,1,0:T(8,128)(2,1)S(1)}, bf16[4,1,32,256]{3,2,1,0:T(8,128)(2,1)S(1)}, u32[]{:S(2)}, u32[]{:S(2)}) collective-permute-start(bf16[4,1,32,256]{3,2,1,0:T(8,128)(2,1)S(1)} %bitcast.203), channel_id=1, source_target_pairs={{0,8},{8,16},{16,24},{24,32},{32,40},{40,48},{48,56},{56,64},{64,7... | collective-permute-start | bytes 196616 | tf_op jit(solution)/shard_map/ppermute | solution.py:27
  135.1 4.2 %collective-permute-start.23 = (bf16[4,1,32,256]{3,2,1,0:T(8,128)(2,1)S(1)}, bf16[4,1,32,256]{3,2,1,0:T(8,128)(2,1)S(1)}, u32[]{:S(2)}, u32[]{:S(2)}) collective-permute-start(bf16[4,1,32,256]{3,2,1,0:T(8,128)(2,1)S(1)} %bitcast.204), channel_id=1, source_target_pairs={{0,16},{8,24},{16,32},{24,40},{32,48},{40,56},{48,64},{56,72},{64,... | collective-permute-start | bytes 196616 | tf_op jit(solution)/shard_map/ppermute | solution.py:27
  (129 shorter events, 50.4 us)
Async XLA Ops:
  0.6 27.2 %collective-permute-start = (bf16[4,1,32,256]{3,2,1,0:T(8,128)(2,1)}, bf16[4,1,32,256]{3,2,1,0:T(8,128)(2,1)}, u32[]{:S(2)}, u32[]{:S(2)}) collective-permute-start(bf16[4,1,32,256]{3,2,1,0:T(8,128)(2,1)} %param.9), channel_id=1, source_target_pairs={{0,16},{8,24},{16,32},{24,40},{32,48},{40,56},{48,64},{56,72},{64,... | collective-permute-start | bytes 196616 | tf_op jit(solution)/shard_map/ppermute | solution.py:27
  6.6 22.1 %collective-permute-start.1 = (bf16[4,1,32,256]{3,2,1,0:T(8,128)(2,1)}, bf16[4,1,32,256]{3,2,1,0:T(8,128)(2,1)}, u32[]{:S(2)}, u32[]{:S(2)}) collective-permute-start(bf16[4,1,32,256]{3,2,1,0:T(8,128)(2,1)} %param.9), channel_id=1, source_target_pairs={{0,8},{8,16},{16,24},{24,32},{32,40},{40,48},{48,56},{56,64},{64,7... | collective-permute-start | bytes 196616 | tf_op jit(solution)/shard_map/ppermute | solution.py:27
  10.7 19.7 %collective-permute-start.2 = (bf16[4,1,32,256]{3,2,1,0:T(8,128)(2,1)}, bf16[4,1,32,256]{3,2,1,0:T(8,128)(2,1)}, u32[]{:S(2)}, u32[]{:S(2)}) collective-permute-start(bf16[4,1,32,256]{3,2,1,0:T(8,128)(2,1)} %param.9), channel_id=1, source_target_pairs={{8,0},{16,8},{24,16},{32,24},{40,32},{48,40},{56,48},{64,56},{72,6... | collective-permute-start | bytes 196616 | tf_op jit(solution)/shard_map/ppermute | solution.py:27
  12.7 18.6 %collective-permute-start.3 = (bf16[4,1,32,256]{3,2,1,0:T(8,128)(2,1)}, bf16[4,1,32,256]{3,2,1,0:T(8,128)(2,1)}, u32[]{:S(2)}, u32[]{:S(2)}) collective-permute-start(bf16[4,1,32,256]{3,2,1,0:T(8,128)(2,1)} %param.9), channel_id=1, source_target_pairs={{16,0},{24,8},{32,16},{40,24},{48,32},{56,40},{64,48},{72,56},{80,... | collective-permute-start | bytes 196616 | tf_op jit(solution)/shard_map/ppermute | solution.py:27
  17.7 23.8 %collective-permute-start.12 = (bf16[1,1,32,256]{3,0,2,1:T(2,128)(2,1)}, bf16[1,1,32,256]{3,0,2,1:T(2,128)(2,1)}, u32[]{:S(2)}, u32[]{:S(2)}) collective-permute-start(bf16[1,1,32,256]{3,0,2,1:T(2,128)(2,1)} %get-tuple-element.21), channel_id=1, source_target_pairs={{0,8},{8,16},{16,24},{24,32},{32,40},{40,48},{48,56},{56,64},{64,7... | collective-permute-start | bytes 49160 | tf_op jit(solution)/shard_map/ppermute | solution.py:15
  35.5 6.1 %collective-permute-start.4 = (bf16[1,1,32,256]{3,0,2,1:T(2,128)(2,1)}, bf16[1,1,32,256]{3,0,2,1:T(2,128)(2,1)}, u32[]{:S(2)}, u32[]{:S(2)}) collective-permute-start(bf16[1,1,32,256]{3,0,2,1:T(2,128)(2,1)} %get-tuple-element.19), channel_id=1, source_target_pairs={{0,8},{8,16},{16,24},{24,32},{32,40},{40,48},{48,56},{56,64},{64,7... | collective-permute-start | bytes 49160 | tf_op jit(solution)/shard_map/ppermute | solution.py:15
  38.4 9.4 %collective-permute-start.5 = (bf16[1,1,32,256]{3,0,2,1:T(2,128)(2,1)}, bf16[1,1,32,256]{3,0,2,1:T(2,128)(2,1)}, u32[]{:S(2)}, u32[]{:S(2)}) collective-permute-start(bf16[1,1,32,256]{3,0,2,1:T(2,128)(2,1)} %get-tuple-element.18), channel_id=1, source_target_pairs={{8,0},{16,8},{24,16},{32,24},{40,32},{48,40},{56,48},{64,56},{72,6... | collective-permute-start | bytes 49160 | tf_op jit(solution)/shard_map/ppermute | solution.py:17
  49.5 22.3 %collective-permute-start.6 = (bf16[11,1,32,256]{3,0,2,1:T(8,128)(2,1)}, bf16[11,1,32,256]{3,0,2,1:T(8,128)(2,1)}, u32[]{:S(2)}, u32[]{:S(2)}) collective-permute-start(bf16[11,1,32,256]{3,0,2,1:T(8,128)(2,1)} %dynamic_update_slice.12), channel_id=1, source_target_pairs={{0,1},{1,2},{2,3},{3,4},{4,5},{5,6},{6,7},{8,9},{9,10},{10,11},{11... | collective-permute-start | bytes 540680 | tf_op jit(solution)/shard_map/ppermute | solution.py:15
  51.4 20.4 %collective-permute-start.7 = (bf16[11,1,32,256]{3,0,2,1:T(8,128)(2,1)}, bf16[11,1,32,256]{3,0,2,1:T(8,128)(2,1)}, u32[]{:S(2)}, u32[]{:S(2)}) collective-permute-start(bf16[11,1,32,256]{3,0,2,1:T(8,128)(2,1)} %dynamic_update_slice.12), channel_id=1, source_target_pairs={{1,0},{2,1},{3,2},{4,3},{5,4},{6,5},{7,6},{9,8},{10,9},{11,10},{12... | collective-permute-start | bytes 540680 | tf_op jit(solution)/shard_map/ppermute | solution.py:17
  55.1 9.4 %collective-permute-start.13 = (bf16[1,1,32,256]{3,0,2,1:T(2,128)(2,1)}, bf16[1,1,32,256]{3,0,2,1:T(2,128)(2,1)}, u32[]{:S(2)}, u32[]{:S(2)}) collective-permute-start(bf16[1,1,32,256]{3,0,2,1:T(2,128)(2,1)} %get-tuple-element.20), channel_id=1, source_target_pairs={{8,0},{16,8},{24,16},{32,24},{40,32},{48,40},{56,48},{64,56},{72,6... | collective-permute-start | bytes 49160 | tf_op jit(solution)/shard_map/ppermute | solution.py:17
  66.2 9.1 %collective-permute-start.14 = (bf16[11,1,32,256]{3,0,2,1:T(8,128)(2,1)}, bf16[11,1,32,256]{3,0,2,1:T(8,128)(2,1)S(1)}, u32[]{:S(2)}, u32[]{:S(2)}) collective-permute-start(bf16[11,1,32,256]{3,0,2,1:T(8,128)(2,1)} %dynamic_update_slice.14), channel_id=1, source_target_pairs={{0,1},{1,2},{2,3},{3,4},{4,5},{5,6},{6,7},{8,9},{9,10},{10,11},{11... | collective-permute-start | bytes 540680 | tf_op jit(solution)/shard_map/ppermute | solution.py:15
  68.1 7.8 %collective-permute-start.15 = (bf16[11,1,32,256]{3,0,2,1:T(8,128)(2,1)}, bf16[11,1,32,256]{3,0,2,1:T(8,128)(2,1)S(1)}, u32[]{:S(2)}, u32[]{:S(2)}) collective-permute-start(bf16[11,1,32,256]{3,0,2,1:T(8,128)(2,1)} %dynamic_update_slice.14), channel_id=1, source_target_pairs={{1,0},{2,1},{3,2},{4,3},{5,4},{6,5},{7,6},{9,8},{10,9},{11,10},{12... | collective-permute-start | bytes 540680 | tf_op jit(solution)/shard_map/ppermute | solution.py:17
  81.1 8.0 %collective-permute-start.8 = (bf16[1,1,32,256]{3,0,2,1:T(2,128)(2,1)S(1)}, bf16[1,1,32,256]{3,0,2,1:T(2,128)(2,1)S(1)}, u32[]{:S(2)}, u32[]{:S(2)}) collective-permute-start(bf16[1,1,32,256]{3,0,2,1:T(2,128)(2,1)S(1)} %get-tuple-element.17), channel_id=1, source_target_pairs={{0,8},{8,16},{16,24},{24,32},{32,40},{40,48},{48,56},{56,64},{64,7... | collective-permute-start | bytes 49160 | tf_op jit(solution)/shard_map/ppermute | solution.py:15
  83.1 6.0 %collective-permute-start.16 = (bf16[1,1,32,256]{3,0,2,1:T(2,128)(2,1)S(1)}, bf16[1,1,32,256]{3,0,2,1:T(2,128)(2,1)S(1)}, u32[]{:S(2)}, u32[]{:S(2)}) collective-permute-start(bf16[1,1,32,256]{3,0,2,1:T(2,128)(2,1)S(1)} %get-tuple-element.15), channel_id=1, source_target_pairs={{0,8},{8,16},{16,24},{24,32},{32,40},{40,48},{48,56},{56,64},{64,7... | collective-permute-start | bytes 49160 | tf_op jit(solution)/shard_map/ppermute | solution.py:15
  85.2 9.2 %collective-permute-start.17 = (bf16[1,1,32,256]{3,0,2,1:T(2,128)(2,1)S(1)}, bf16[1,1,32,256]{3,0,2,1:T(2,128)(2,1)}, u32[]{:S(2)}, u32[]{:S(2)}) collective-permute-start(bf16[1,1,32,256]{3,0,2,1:T(2,128)(2,1)S(1)} %get-tuple-element.14), channel_id=1, source_target_pairs={{8,0},{16,8},{24,16},{32,24},{40,32},{48,40},{56,48},{64,56},{72,6... | collective-permute-start | bytes 49160 | tf_op jit(solution)/shard_map/ppermute | solution.py:17
  96.1 22.5 %collective-permute-start.18 = (bf16[11,1,32,256]{3,0,2,1:T(8,128)(2,1)}, bf16[11,1,32,256]{3,0,2,1:T(8,128)(2,1)}, u32[]{:S(2)}, u32[]{:S(2)}) collective-permute-start(bf16[11,1,32,256]{3,0,2,1:T(8,128)(2,1)} %dynamic_update_slice.15), channel_id=1, source_target_pairs={{0,1},{1,2},{2,3},{3,4},{4,5},{5,6},{6,7},{8,9},{9,10},{10,11},{11... | collective-permute-start | bytes 540680 | tf_op jit(solution)/shard_map/ppermute | solution.py:15
  98.5 20.1 %collective-permute-start.19 = (bf16[11,1,32,256]{3,0,2,1:T(8,128)(2,1)}, bf16[11,1,32,256]{3,0,2,1:T(8,128)(2,1)}, u32[]{:S(2)}, u32[]{:S(2)}) collective-permute-start(bf16[11,1,32,256]{3,0,2,1:T(8,128)(2,1)} %dynamic_update_slice.15), channel_id=1, source_target_pairs={{1,0},{2,1},{3,2},{4,3},{5,4},{6,5},{7,6},{9,8},{10,9},{11,10},{12... | collective-permute-start | bytes 540680 | tf_op jit(solution)/shard_map/ppermute | solution.py:17
  101.7 9.4 %collective-permute-start.9 = (bf16[1,1,32,256]{3,0,2,1:T(2,128)(2,1)}, bf16[1,1,32,256]{3,0,2,1:T(2,128)(2,1)}, u32[]{:S(2)}, u32[]{:S(2)}) collective-permute-start(bf16[1,1,32,256]{3,0,2,1:T(2,128)(2,1)} %get-tuple-element.16), channel_id=1, source_target_pairs={{8,0},{16,8},{24,16},{32,24},{40,32},{48,40},{56,48},{64,56},{72,6... | collective-permute-start | bytes 49160 | tf_op jit(solution)/shard_map/ppermute | solution.py:17
  112.8 22.2 %collective-permute-start.10 = (bf16[11,1,32,256]{3,0,2,1:T(8,128)(2,1)}, bf16[11,1,32,256]{3,0,2,1:T(8,128)(2,1)S(1)}, u32[]{:S(2)}, u32[]{:S(2)}) collective-permute-start(bf16[11,1,32,256]{3,0,2,1:T(8,128)(2,1)} %dynamic_update_slice.13), channel_id=1, source_target_pairs={{0,1},{1,2},{2,3},{3,4},{4,5},{5,6},{6,7},{8,9},{9,10},{10,11},{11... | collective-permute-start | bytes 540680 | tf_op jit(solution)/shard_map/ppermute | solution.py:15
  114.8 24.6 %collective-permute-start.11 = (bf16[11,1,32,256]{3,0,2,1:T(8,128)(2,1)}, bf16[11,1,32,256]{3,0,2,1:T(8,128)(2,1)S(1)}, u32[]{:S(2)}, u32[]{:S(2)}) collective-permute-start(bf16[11,1,32,256]{3,0,2,1:T(8,128)(2,1)} %dynamic_update_slice.13), channel_id=1, source_target_pairs={{1,0},{2,1},{3,2},{4,3},{5,4},{6,5},{7,6},{9,8},{10,9},{11,10},{12... | collective-permute-start | bytes 540680 | tf_op jit(solution)/shard_map/ppermute | solution.py:17
  123.9 20.1 %collective-permute-start.20 = (bf16[4,1,32,256]{3,2,1,0:T(8,128)(2,1)S(1)}, bf16[4,1,32,256]{3,2,1,0:T(8,128)(2,1)S(1)}, u32[]{:S(2)}, u32[]{:S(2)}) collective-permute-start(bf16[4,1,32,256]{3,2,1,0:T(8,128)(2,1)S(1)} %bitcast.201), channel_id=1, source_target_pairs={{16,0},{24,8},{32,16},{40,24},{48,32},{56,40},{64,48},{72,56},{80,... | collective-permute-start | bytes 196616 | tf_op jit(solution)/shard_map/ppermute | solution.py:27
  125.9 18.1 %collective-permute-start.21 = (bf16[4,1,32,256]{3,2,1,0:T(8,128)(2,1)S(1)}, bf16[4,1,32,256]{3,2,1,0:T(8,128)(2,1)S(1)}, u32[]{:S(2)}, u32[]{:S(2)}) collective-permute-start(bf16[4,1,32,256]{3,2,1,0:T(8,128)(2,1)S(1)} %bitcast.202), channel_id=1, source_target_pairs={{8,0},{16,8},{24,16},{32,24},{40,32},{48,40},{56,48},{64,56},{72,6... | collective-permute-start | bytes 196616 | tf_op jit(solution)/shard_map/ppermute | solution.py:27
  127.8 16.2 %collective-permute-start.22 = (bf16[4,1,32,256]{3,2,1,0:T(8,128)(2,1)S(1)}, bf16[4,1,32,256]{3,2,1,0:T(8,128)(2,1)S(1)}, u32[]{:S(2)}, u32[]{:S(2)}) collective-permute-start(bf16[4,1,32,256]{3,2,1,0:T(8,128)(2,1)S(1)} %bitcast.203), channel_id=1, source_target_pairs={{0,8},{8,16},{16,24},{24,32},{32,40},{40,48},{48,56},{56,64},{64,7... | collective-permute-start | bytes 196616 | tf_op jit(solution)/shard_map/ppermute | solution.py:27
  135.1 8.9 %collective-permute-start.23 = (bf16[4,1,32,256]{3,2,1,0:T(8,128)(2,1)S(1)}, bf16[4,1,32,256]{3,2,1,0:T(8,128)(2,1)S(1)}, u32[]{:S(2)}, u32[]{:S(2)}) collective-permute-start(bf16[4,1,32,256]{3,2,1,0:T(8,128)(2,1)S(1)} %bitcast.204), channel_id=1, source_target_pairs={{0,16},{8,24},{16,32},{24,40},{32,48},{40,56},{48,64},{56,72},{64,... | collective-permute-start | bytes 196616 | tf_op jit(solution)/shard_map/ppermute | solution.py:27
  (20 other events, 137.6 us)
where the time goes:
time: 146 us; the launch traced here: 145 us
  starting transfers between devices  76.2 us (52%)
  waiting for transfers between devices  24.1 us (17%)
  local copies, waits for them, and re-layouts  24 us (16%)
  other arithmetic  9.4 us (6%)
  matrix products  8.83 us (6%)
  between operations  2.1 us (1%)
    ppermute x8, starting transfers between devices, from_behind(): return lax.ppermute(x, axis, pairs)  29.2 us
    ppermute x8, starting transfers between devices, extended_2(): lax.ppermute(head, axis, [((i + 1) % count, i) for i in range(ends)])  25.1 us
    ppermute x8, waiting for transfers between devices, extended_2(): lax.ppermute(head, axis, [((i + 1) % count, i) for i in range(ends)])  23.9 us
    ppermute x8, starting transfers between devices, extended_2(): lax.ppermute(tail, axis, [(i, (i + 1) % count) for i in range(ends)])  22 us
    unnamed x53, local copies, waits for them, and re-layouts  11.8 us
    dynamic_update_slice x4, local copies, waits for them, and re-layouts, surround(): lax.dynamic_update_slice_in_dim(extended, edges[3:], filled + 1, 0)  6.79 us
    conv_general_dilated x4, matrix products, convolve(): lax.conv_general_dilated(extended[None], kernel, (1, 1, 1), 'VALID', dime...  5.97 us
    concatenate x2, other arithmetic, surround(): extended = jnp.concatenate([edges[:1], slab, jnp.zeros_like(slab[:1])], 0)  3.2 us
  transfers between devices with their start and end apart: 24, of which 6 were waited for; matrix products, arithmetic and copies ran while one was open for 20% of the time, Pallas kernels for 0%

commit v1 on v0

v1 whole, which is shorter than its diff:
```python
import jax
import jax.numpy as jnp
from jax import lax
from jax.experimental import pallas as pl
from jax.experimental.pallas import tpu as pltpu
from jax.sharding import PartitionSpec as P

MESH = pl.DeviceIdType.MESH
FRAMES = 4
CAP = 9
TAPS = 4
WINDOW = 16
BELOW = 6
W = 32
C = 256
OWN, NEAR, FAR = 0, 1, 2
BF16 = jnp.bfloat16
F32 = jnp.float32


def kernel(
    spans,
    lines,
    source,
    counts,
    frames,
    weights,
    kernel_one,
    bias_one,
    kernel_two,
    bias_two,
    upstream,
    decoded,
    source_grad,
    window,
    w_one,
    w_two,
    b_one,
    b_two,
    raw,
    blended,
    first,
    middle,
    low,
    back_two,
    parts,
    inc,
    act_one,
    grad_mid,
    act_two,
    inc_edge,
    act_one_edge,
    grad_mid_edge,
    act_two_edge,
    last,
    spread,
    arrived,
    total,
    result,
    mix,
    c_s,
    f_s,
    w_s,
    local,
    send,
    recv,
):
    d = lax.axis_index("tm")
    r = lax.axis_index("rows")
    odd = lax.rem(r, 2)
    near = r + 1 - 2 * odd
    far = lax.rem(r - 1 + 2 * odd + lines, lines)
    far_there = jnp.where(odd == 0, r > 0, r < lines - 1)
    near_tap = 2 - 2 * odd
    far_tap = 2 * odd

    def span(by):
        return lax.rem(d + by + spans, spans)

    reach = [(by, r) for by in (-2, -1, 1, 2)] + [(0, near), (0, far)]
    reach += [(by, row) for by in (-1, 1) for row in (near, far)]
    barrier = pltpu.get_barrier_semaphore()
    for by, row in reach:
        pl.semaphore_signal(
            barrier, inc=1, device_id={"tm": span(by), "rows": row}, device_id_type=MESH
        )

    def fetch(k, src, dst):
        copy = pltpu.make_async_copy(src, dst, local.at[k])
        copy.start()
        return copy

    get_source = fetch(0, source, window.at[pl.ds(BELOW, FRAMES)])
    get_counts = fetch(1, counts, c_s)
    get_frames = fetch(2, frames, f_s)
    get_weights = fetch(3, weights, w_s)
    get_raw = fetch(4, upstream, raw)
    get_two = fetch(5, kernel_two, w_two)
    get_one = fetch(6, kernel_one, w_one)
    get_b_one = fetch(7, bias_one, b_one)
    get_b_two = fetch(8, bias_two, b_two)

    copies = []

    def push(src, dst, by, row):
        k = len(copies)
        copy = pltpu.make_async_remote_copy(
            src_ref=src,
            dst_ref=dst,
            send_sem=send.at[k],
            recv_sem=recv.at[k],
            device_id={"tm": span(by), "rows": row},
            device_id_type=MESH,
        )
        copy.start()
        copies.append(copy)
        return copy

    def exchange(box, edge, ends):
        mine = box.at[OWN, pl.ds(1, CAP)]
        head = box.at[OWN, 1]
        return [
            push(mine, box.at[FAR, pl.ds(1, CAP)], 0, far),
            push(ends, box.at[FAR, 0], 1, far),
            push(head, edge.at[FAR], -1, far),
            push(ends, box.at[OWN, 0], 1, r),
            push(head, edge.at[OWN], -1, r),
            push(ends, box.at[NEAR, 0], 1, near),
            push(head, edge.at[NEAR], -1, near),
            push(mine, box.at[NEAR, pl.ds(1, CAP)], 0, near),
        ]

    get_source.wait()
    pl.semaphore_wait(barrier, len(reach))
    sources = [
        push(window.at[pl.ds(BELOW, 4)], window.at[pl.ds(2, 4)], 1, r),
        push(window.at[pl.ds(BELOW, 4)], window.at[pl.ds(10, 4)], -1, r),
        push(window.at[pl.ds(BELOW + 2, 2)], window.at[pl.ds(0, 2)], 2, r),
        push(window.at[pl.ds(BELOW, 2)], window.at[pl.ds(14, 2)], -2, r),
    ]

    get_counts.wait()
    get_frames.wait()
    get_weights.wait()
    filled = c_s[0]
    lowest = d * FRAMES - BELOW
    used = [j < filled for j in range(CAP)]
    none = jnp.zeros((W, C), BF16)

    get_raw.wait()
    for j in range(CAP):
        inc[OWN, 1 + j] = jnp.where(used[j], raw[j], none)
    last[0] = raw[jnp.clip(filled - 1, 0, CAP - 1)]
    inc_copies = exchange(inc, inc_edge, last.at[0])

    for j in range(CAP):
        for f in range(WINDOW):
            weight = jnp.float32(0.0)
            for k in range(TAPS):
                weight += jnp.where(f_s[j, k] == lowest + f, w_s[j, k], 0.0)
            mix[j, f] = jnp.where(used[j], weight, 0.0)

    for copy in sources:
        copy.wait_recv()
    for j in range(CAP):
        summed = jnp.zeros((W, C), F32)
        for k in range(TAPS):
            at = jnp.clip(f_s[j, k] - lowest, 0, WINDOW - 1)
            summed += w_s[j, k] * window[at].astype(F32)
        value = jnp.where(used[j], summed, 0.0).astype(BF16)
        blended[j] = value
        wide = value.astype(F32)
        value = (wide * jax.nn.sigmoid(wide)).astype(BF16)
        act_one[OWN, 1 + j] = value
        end = value if j == 0 else jnp.where(filled == j + 1, value, end)
    last[1] = end
    act_one_copies = exchange(act_one, act_one_edge, last.at[1])

    def settle(box, edge):
        for s in (OWN, NEAR, FAR):
            there = far_there if s == FAR else None
            before = d > 0 if there is None else (d > 0) & there
            after = d < spans - 1 if there is None else (d < spans - 1) & there
            box[s, 0] = jnp.where(before, box[s, 0], none)
            follow = jnp.where(after, edge[s], none)
            if s == FAR:
                box[s, 1] = jnp.where(there, box[s, 1], none)
            for e in range(2, CAP + 2):
                held = box[s, e] if e <= CAP else none
                if s == FAR:
                    held = jnp.where(there, held, none)
                box[s, e] = jnp.where(filled + 1 == e, follow, held)

    def convolve(box, w, back):
        taps = (1, near_tap, far_tap)
        for s in (OWN, NEAR, FAR):
            fields = jnp.concatenate(
                [box[s, a : a + CAP].reshape(CAP * W, C) for a in range(3)], axis=1
            )
            for c in range(3):
                if back:
                    tile = jnp.concatenate([w[2 - a, 2 - taps[s], 2 - c] for a in range(3)], axis=1)
                    dims = (((1,), (1,)), ((), ()))
                else:
                    tile = jnp.concatenate([w[a, taps[s], c] for a in range(3)], axis=0)
                    dims = (((1,), (0,)), ((), ()))
                term = lax.dot_general(fields, tile, dims, preferred_element_type=F32)
                if s == OWN:
                    parts[c] = term
                else:
                    parts[c] += term

    column = lax.broadcasted_iota(jnp.int32, (W, C), 0)

    def joined(j):
        rows = pl.ds(j * W, W)
        left = jnp.where(column == 0, 0.0, pltpu.roll(parts[0, rows], 1, 0))
        right = jnp.where(column == W - 1, 0.0, pltpu.roll(parts[2, rows], W - 1, 0))
        return parts[1, rows] + left + right

    for copy in inc_copies:
        copy.wait()
    settle(inc, inc_edge)
    get_two.wait()
    convolve(inc, w_two, True)
    for j in range(CAP):
        back_two[j] = joined(j)

    for copy in act_one_copies:
        copy.wait()
    settle(act_one, act_one_edge)
    get_one.wait()
    get_b_one.wait()
    get_b_two.wait()
    convolve(act_one, w_one, False)
    for j in range(CAP):
        value = blended[j].astype(F32) + joined(j) + b_one[...]
        value = jnp.where(used[j], value, 0.0).astype(BF16)
        first[j] = value
        wide = value.astype(F32)
        gate = jax.nn.sigmoid(wide)
        act = (wide * gate).astype(BF16)
        act_two[OWN, 1 + j] = act
        slope = gate * (1.0 + wide * (1.0 - gate))
        given = jnp.where(used[j], raw[j], none).astype(F32)
        value = given + slope * back_two[j]
        value = jnp.where(used[j], value, 0.0).astype(BF16)
        grad_mid[OWN, 1 + j] = value
        end_mid = value if j == 0 else jnp.where(filled == j + 1, value, end_mid)
        end_two = act if j == 0 else jnp.where(filled == j + 1, act, end_two)
    last[2] = end_mid
    grad_mid_copies = exchange(grad_mid, grad_mid_edge, last.at[2])
    last[3] = end_two
    act_two_copies = exchange(act_two, act_two_edge, last.at[3])

    for copy in grad_mid_copies:
        copy.wait()
    settle(grad_mid, grad_mid_edge)
    convolve(grad_mid, w_one, True)
    for j in range(CAP):
        wide = blended[j].astype(F32)
        gate = jax.nn.sigmoid(wide)
        slope = gate * (1.0 + wide * (1.0 - gate))
        low[j] = grad_mid[OWN, 1 + j].astype(F32) * jnp.where(used[j], 1.0, 0.0) + slope * joined(j)
    for f in range(WINDOW):
        summed = mix[0, f] * low[0]
        for j in range(1, CAP):
            summed += mix[j, f] * low[j]
        if BELOW <= f < BELOW + FRAMES:
            total[f - BELOW] = summed
        else:
            spread[f] = summed.astype(BF16)
    spread_copies = [
        push(spread.at[pl.ds(2, 4)], arrived.at[pl.ds(0, 4)], -1, r),
        push(spread.at[pl.ds(10, 4)], arrived.at[pl.ds(4, 4)], 1, r),
        push(spread.at[pl.ds(0, 2)], arrived.at[pl.ds(8, 2)], -2, r),
        push(spread.at[pl.ds(14, 2)], arrived.at[pl.ds(10, 2)], 2, r),
    ]

    for copy in act_two_copies:
        copy.wait()
    settle(act_two, act_two_edge)
    convolve(act_two, w_two, False)
    for j in range(CAP):
        value = first[j].astype(F32) + joined(j) + b_two[...]
        result[j] = jnp.where(used[j], value, 0.0).astype(BF16)
    put_decoded = fetch(9, result, decoded)

    for copy in spread_copies:
        copy.wait_recv()
    for f in range(FRAMES):
        value = total[f] + arrived[f].astype(F32) + arrived[4 + f].astype(F32)
        if f >= 2:
            value += arrived[8 + f - 2].astype(F32)
        else:
            value += arrived[10 + f].astype(F32)
        total[f] = value
    put_grad = fetch(10, total, source_grad)
    for copy in sources + spread_copies:
        copy.wait_send()
    put_decoded.wait()
    put_grad.wait()


def solution(mesh):
    spans, lines = mesh.shape["tm"], mesh.shape["rows"]

    def body(
        source,
        frame_counts,
        tap_frames,
        tap_weights,
        kernel_one,
        bias_one,
        kernel_two,
        bias_two,
        upstream,
    ):
        box = pltpu.VMEM((3, CAP + 2, W, C), BF16)
        edge = pltpu.VMEM((3, W, C), BF16)
        slots = pltpu.VMEM((CAP, W, C), BF16)
        wide_slots = pltpu.VMEM((CAP, W, C), F32)
        kernels = pltpu.VMEM((3, 3, 3, C, C), BF16)
        bias = pltpu.VMEM((1, C), F32)
        decoded, source_grad = pl.pallas_call(
            lambda *refs: kernel(spans, lines, *refs),
            out_shape=(
                jax.ShapeDtypeStruct((CAP, W, C), BF16),
                jax.ShapeDtypeStruct((FRAMES, W, C), F32),
            ),
            in_specs=[pl.BlockSpec(memory_space=pl.ANY)] * 9,
            out_specs=[pl.BlockSpec(memory_space=pl.ANY)] * 2,
            scratch_shapes=[
                pltpu.VMEM((WINDOW, W, C), BF16),
                kernels,
                kernels,
                bias,
                bias,
                slots,
                slots,
                slots,
                slots,
                wide_slots,
                wide_slots,
                pltpu.VMEM((3, CAP * W, C), F32),
                box,
                box,
                box,
                box,
                edge,
                edge,
                edge,
                edge,
                pltpu.VMEM((4, W, C), BF16),
                pltpu.VMEM((WINDOW, W, C), BF16),
                pltpu.VMEM((12, W, C), BF16),
                pltpu.VMEM((FRAMES, W, C), F32),
                slots,
                pltpu.SMEM((CAP, WINDOW), F32),
                pltpu.SMEM((1,), jnp.int32),
                pltpu.SMEM((CAP, TAPS), jnp.int32),
                pltpu.SMEM((CAP, TAPS), F32),
                pltpu.SemaphoreType.DMA((11,)),
                pltpu.SemaphoreType.DMA((40,)),
                pltpu.SemaphoreType.DMA((40,)),
            ],
            compiler_params=pltpu.CompilerParams(
                collective_id=0, has_side_effects=True, vmem_limit_bytes=48 * 1024 * 1024
            ),
            cost_estimate=pl.CostEstimate(
                flops=4 * 2 * CAP * W * 27 * C * C,
                bytes_accessed=2 * 27 * C * C * 2,
                transcendentals=0,
            ),
        )(
            source.reshape(FRAMES, W, C),
            frame_counts,
            tap_frames,
            tap_weights,
            kernel_one,
            bias_one.reshape(1, C),
            kernel_two,
            bias_two.reshape(1, C),
            upstream.reshape(CAP, W, C),
        )
        return decoded.reshape(CAP, 1, W, C), source_grad.reshape(FRAMES, 1, W, C)

    whole = P("tm", "rows", None, None)
    return jax.shard_map(
        body,
        mesh=mesh,
        in_specs=(whole, P("tm"), P("tm", None), P("tm", None), P(), P(), P(), P(), whole),
        out_specs=(whole, whole),
        check_vma=False,
    )
```

time: 146 us -> 46.4 us (0.32)
  the two profiles are of different devices: /device:TPU:122 before, /device:TPU:1 now
where the time goes in v1:
time: 46.4 us; the launch traced here: 46.1 us
  Pallas kernels  36.9 us (80%)
  local copies, waits for them, and re-layouts  7.96 us (17%)
  between operations  1.29 us (3%)
    pallas_call x1, Pallas kernels, body(): pl.pallas_call(lambda *refs: kernel(spans, lines, *refs), out_shape=(jax....  36.9 us
    unnamed x14, local copies, waits for them, and re-layouts  7.96 us

profile of v1, /device:TPU:1, one launch (start us, length us, event | category | flops | bytes accessed | tf_op | source)
XLA Modules:
  0.0 46.1 jit_solution(7834550487542757095)
XLA Ops:
  1.3 0.8 %copy.11.refs_2_ = s32[9,4]{1,0:T(8,128)S(1)} copy(s32[9,4]{0,1:T(4,128)} %param.11) | data formatting | bytes 288 | tf_op args[2]
  2.0 0.8 %copy.12.refs_3_ = f32[9,4]{1,0:T(8,128)S(1)} copy(f32[9,4]{0,1:T(4,128)} %param.12) | data formatting | bytes 288 | tf_op args[3]
  2.8 0.0 copy-start
  2.8 2.0 %copy-done = bf16[3,3,3,256,256]{4,3,2,1,0:T(8,128)(2,1)S(1)} copy-done((bf16[3,3,3,256,256]{4,3,2,1,0:T(8,128)(2,1)S(1)}, bf16[3,3,3,256,256]{4,3,2,1,0:T(8,128)(2,1)}, u32[]{:S(2)}) %copy-start) | copy-done | bytes 3538968
  4.8 0.0 copy-start.1
  4.8 0.9 %copy-done.1 = bf16[9,1,32,256]{3,2,1,0:T(8,128)(2,1)S(1)} copy-done((bf16[9,1,32,256]{3,2,1,0:T(8,128)(2,1)S(1)}, bf16[9,1,32,256]{3,2,1,0:T(8,128)(2,1)}, u32[]{:S(2)}) %copy-start.1) | copy-done | bytes 147480
  5.7 0.0 copy-start.2
  5.7 0.8 %copy-done.2 = bf16[4,1,32,256]{3,2,1,0:T(8,128)(2,1)S(1)} copy-done((bf16[4,1,32,256]{3,2,1,0:T(8,128)(2,1)S(1)}, bf16[4,1,32,256]{3,2,1,0:T(8,128)(2,1)}, u32[]{:S(2)}) %copy-start.2) | copy-done | bytes 65560
  6.6 0.0 copy-start.3
  6.6 0.7 %copy-done.3 = f32[256]{0:T(256)S(1)} copy-done((f32[256]{0:T(256)S(1)}, f32[256]{0:T(256)}, u32[]{:S(2)}) %copy-start.3) | copy-done | bytes 1048
  7.2 0.0 copy-start.4
  7.2 0.7 %copy-done.4 = f32[256]{0:T(256)S(1)} copy-done((f32[256]{0:T(256)S(1)}, f32[256]{0:T(256)}, u32[]{:S(2)}) %copy-start.4) | copy-done | bytes 1048
  7.9 36.9 %shard_map.104 = (bf16[9,32,256]{2,1,0:T(8,128)(2,1)S(1)}, f32[4,32,256]{2,1,0:T(8,128)S(1)}) custom-call(bf16[4,32,256]{2,1,0:T(8,128)(2,1)S(1)} %bitcast.13, s32[1]{0:T(128)S(6)} %copy.17.refs_1_, s32[9,4]{1,0:T(8,128)S(1)} %copy.11.refs_2_, f32[9,4]{1,0:T(8,128)S(1)} %copy.12.refs_3_, bf16[3,3,3,256,256]{4,3,2,1,0:T(8,128)(2,1)S(1)} %copy-done, ...), custom_call_target="tpu_custom_call" | custom-call | flops 4076863488 | bytes 7077888 | tf_op jit(solution)/shard_map/pallas_call | solution.py:325
  44.8 0.7 %copy.18 = bf16[9,1,32,256]{3,2,1,0:T(8,128)(2,1)} copy(bf16[9,1,32,256]{3,2,1,0:T(8,128)(2,1)S(1)} %bitcast.10) | data formatting | bytes 294912
  45.5 0.7 %copy.19 = f32[4,1,32,256]{3,2,1,0:T(8,128)} copy(f32[4,1,32,256]{3,2,1,0:T(8,128)S(1)} %bitcast.11) | data formatting | bytes 262144
Async XLA Ops:
  2.8 2.0 %copy-start = (bf16[3,3,3,256,256]{4,3,2,1,0:T(8,128)(2,1)S(1)}, bf16[3,3,3,256,256]{4,3,2,1,0:T(8,128)(2,1)}, u32[]{:S(2)}) copy-start(bf16[3,3,3,256,256]{4,3,2,1,0:T(8,128)(2,1)} %refs_4_.1) | copy-start | bytes 10616836
  4.8 0.9 %copy-start.1 = (bf16[9,1,32,256]{3,2,1,0:T(8,128)(2,1)S(1)}, bf16[9,1,32,256]{3,2,1,0:T(8,128)(2,1)}, u32[]{:S(2)}) copy-start(bf16[9,1,32,256]{3,2,1,0:T(8,128)(2,1)} %param.17) | copy-start | bytes 442372
  5.7 0.8 %copy-start.2 = (bf16[4,1,32,256]{3,2,1,0:T(8,128)(2,1)S(1)}, bf16[4,1,32,256]{3,2,1,0:T(8,128)(2,1)}, u32[]{:S(2)}) copy-start(bf16[4,1,32,256]{3,2,1,0:T(8,128)(2,1)} %param.9) | copy-start | bytes 196612
  6.6 0.7 %copy-start.3 = (f32[256]{0:T(256)S(1)}, f32[256]{0:T(256)}, u32[]{:S(2)}) copy-start(f32[256]{0:T(256)} %param.14) | copy-start | bytes 3076
  7.2 0.7 %copy-start.4 = (f32[256]{0:T(256)S(1)}, f32[256]{0:T(256)}, u32[]{:S(2)}) copy-start(f32[256]{0:T(256)} %param.16) | copy-start | bytes 3076

commit v2 on v1

v2 whole, which is shorter than its diff:
```python
import jax
import jax.numpy as jnp
from jax import lax
from jax.experimental import pallas as pl
from jax.experimental.pallas import tpu as pltpu
from jax.sharding import PartitionSpec as P

MESH = pl.DeviceIdType.MESH
FRAMES = 4
CAP = 9
TAPS = 4
WINDOW = 16
BELOW = 6
W = 32
C = 256
OWN, NEAR, FAR = 0, 1, 2
BF16 = jnp.bfloat16
F32 = jnp.float32


def kernel(
    spans,
    lines,
    source,
    counts,
    frames,
    weights,
    kernel_one,
    bias_one,
    kernel_two,
    bias_two,
    upstream,
    decoded,
    source_grad,
    window,
    w_one,
    w_two,
    b_one,
    b_two,
    raw,
    blended,
    first,
    low,
    back_two,
    slope_one,
    parts,
    inc,
    act_one,
    grad_mid,
    act_two,
    inc_edge,
    act_one_edge,
    grad_mid_edge,
    act_two_edge,
    last,
    spread,
    arrived,
    mix,
    c_s,
    f_s,
    w_s,
    local,
    send,
    recv,
):
    d = lax.axis_index("tm")
    r = lax.axis_index("rows")
    odd = lax.rem(r, 2)
    near = r + 1 - 2 * odd
    far = lax.rem(r - 1 + 2 * odd + lines, lines)
    far_there = jnp.where(odd == 0, r > 0, r < lines - 1)
    near_tap = 2 - 2 * odd
    far_tap = 2 * odd

    upper = spans - 1

    def exists(by):
        if by == 0:
            return None
        return d >= -by if by < 0 else d <= upper - by

    def both(one, two):
        if one is None or two is None:
            return two if one is None else one
        return one & two

    def when(condition, action):
        if condition is None:
            action()
        else:
            pl.when(condition)(action)

    def line(row):
        return far_there if row is far else None

    reach = [(by, r) for by in (-2, -1, 1, 2)] + [(0, near), (0, far)]
    reach += [(by, row) for by in (-1, 1) for row in (near, far)]
    barrier = pltpu.get_barrier_semaphore()
    greeted = jnp.int32(0)
    for by, row in reach:
        there = both(exists(by), line(row))

        def greet(by=by, row=row):
            pl.semaphore_signal(
                barrier, inc=1, device_id={"tm": d + by, "rows": row}, device_id_type=MESH
            )

        when(there, greet)
        greeted += 1 if there is None else jnp.where(there, 1, 0)

    def fetch(k, src, dst):
        copy = pltpu.make_async_copy(src, dst, local.at[k])
        copy.start()
        fetched.append(copy)
        return copy

    fetched = []
    get_source = fetch(0, source, window.at[pl.ds(BELOW, FRAMES)])
    get_raw = fetch(4, upstream, raw)
    get_counts = fetch(1, counts, c_s)
    get_frames = fetch(2, frames, f_s)
    get_weights = fetch(3, weights, w_s)
    get_two = fetch(5, kernel_two, w_two)
    get_one = fetch(6, kernel_one, w_one)
    get_b_one = fetch(7, bias_one, b_one)
    get_b_two = fetch(8, bias_two, b_two)

    copies = []

    def push(src, dst, by, row):
        k = len(copies)
        copy = pltpu.make_async_remote_copy(
            src_ref=src,
            dst_ref=dst,
            send_sem=send.at[k],
            recv_sem=recv.at[k],
            device_id={"tm": d + by, "rows": row},
            device_id_type=MESH,
        )
        when(both(exists(by), line(row)), copy.start)
        entry = [copy, both(exists(by), line(row)), both(exists(-by), line(row)), True, True]
        copies.append(entry)
        return entry

    def landed(*entries):
        for entry in entries:
            if entry[4]:
                when(entry[2], entry[0].wait_recv)
                entry[4] = False

    def left(*entries):
        for entry in entries:
            if entry[3]:
                when(entry[1], entry[0].wait_send)
                entry[3] = False

    def exchange(box, edge, ends):
        mine = box.at[OWN, pl.ds(1, CAP)]
        head = box.at[OWN, 1]
        far_last = push(ends, box.at[FAR, 0], 1, far)
        far_head = push(head, edge.at[FAR], -1, far)
        own_last = push(ends, box.at[OWN, 0], 1, r)
        own_head = push(head, edge.at[OWN], -1, r)
        far_mine = push(mine, box.at[FAR, pl.ds(1, CAP)], 0, far)
        near_last = push(ends, box.at[NEAR, 0], 1, near)
        near_head = push(head, edge.at[NEAR], -1, near)
        near_mine = push(mine, box.at[NEAR, pl.ds(1, CAP)], 0, near)
        out = (far_head, own_head, near_head, far_mine, near_mine)
        return (
            (own_last, own_head),
            (near_last, near_head, near_mine),
            (far_last, far_head, far_mine),
            out,
        )

    get_source.wait()
    pl.semaphore_wait(barrier, greeted)
    sources = [
        push(window.at[pl.ds(BELOW + 2, 2)], window.at[pl.ds(0, 2)], 2, r),
        push(window.at[pl.ds(BELOW, 2)], window.at[pl.ds(14, 2)], -2, r),
        push(window.at[pl.ds(BELOW, 4)], window.at[pl.ds(2, 4)], 1, r),
        push(window.at[pl.ds(BELOW, 4)], window.at[pl.ds(10, 4)], -1, r),
    ]

    get_counts.wait()
    filled = c_s[0]
    lowest = d * FRAMES - BELOW
    used = [j < filled for j in range(CAP)]
    none = jnp.zeros((W, C), BF16)

    get_raw.wait()
    for j in range(CAP):
        inc[OWN, 1 + j] = jnp.where(used[j], raw[j], none)
    last[0] = raw[jnp.clip(filled - 1, 0, CAP - 1)]
    inc_copies = exchange(inc, inc_edge, last.at[0])

    get_frames.wait()
    get_weights.wait()
    landed(*sources)
    for j in range(CAP):
        summed = jnp.zeros((W, C), F32)
        for k in range(TAPS):
            at = jnp.clip(f_s[k, j] - lowest, 0, WINDOW - 1)
            summed += w_s[k, j] * window[at].astype(F32)
        value = jnp.where(used[j], summed, 0.0).astype(BF16)
        blended[j] = value
        wide = value.astype(F32)
        value = (wide * jax.nn.sigmoid(wide)).astype(BF16)
        act_one[OWN, 1 + j] = value
        end = value if j == 0 else jnp.where(filled == j + 1, value, end)
    last[1] = end
    act_one_copies = exchange(act_one, act_one_edge, last.at[1])

    for j in range(CAP):
        for f in range(WINDOW):
            weight = jnp.float32(0.0)
            for k in range(TAPS):
                weight += jnp.where(f_s[k, j] == lowest + f, w_s[k, j], 0.0)
            mix[j, f] = jnp.where(used[j], weight, 0.0)

    def settle(s, box, edge):
        there = far_there if s == FAR else None
        before = both(exists(-1), there)
        after = both(exists(1), there)
        box[s, 0] = jnp.where(before, box[s, 0], none)
        follow = jnp.where(after, edge[s], none)
        if s == FAR:
            box[s, 1] = jnp.where(there, box[s, 1], none)
        for e in range(2, CAP + 2):
            held = box[s, e] if e <= CAP else none
            if s == FAR:
                held = jnp.where(there, held, none)
            box[s, e] = jnp.where(filled + 1 == e, follow, held)

    def convolve(copied, box, edge, w, back):
        taps = (1, near_tap, far_tap)
        left(*copied[3])
        for s in (OWN, NEAR, FAR):
            landed(*copied[s])
            settle(s, box, edge)
            fields = jnp.concatenate(
                [box[s, a : a + CAP].reshape(CAP * W, C) for a in range(3)], axis=1
            )
            for c in range(3):
                if back:
                    tile = jnp.concatenate([w[2 - a, 2 - taps[s], 2 - c] for a in range(3)], axis=1)
                    dims = (((1,), (1,)), ((), ()))
                else:
                    tile = jnp.concatenate([w[a, taps[s], c] for a in range(3)], axis=0)
                    dims = (((1,), (0,)), ((), ()))
                term = lax.dot_general(fields, tile, dims, preferred_element_type=F32)
                if s == OWN:
                    parts[c] = term
                else:
                    parts[c] += term

    column = lax.broadcasted_iota(jnp.int32, (W, C), 0)

    def joined(j):
        rows = pl.ds(j * W, W)
        before = jnp.where(column == 0, 0.0, pltpu.roll(parts[0, rows], 1, 0))
        after = jnp.where(column == W - 1, 0.0, pltpu.roll(parts[2, rows], W - 1, 0))
        return parts[1, rows] + before + after

    get_two.wait()
    convolve(inc_copies, inc, inc_edge, w_two, True)
    for j in range(CAP):
        back_two[j] = joined(j)

    get_one.wait()
    get_b_one.wait()
    get_b_two.wait()
    convolve(act_one_copies, act_one, act_one_edge, w_one, False)
    for j in range(CAP):
        value = blended[j].astype(F32) + joined(j) + b_one[...]
        value = jnp.where(used[j], value, 0.0).astype(BF16)
        first[j] = value
        wide = value.astype(F32)
        gate = jax.nn.sigmoid(wide)
        slope = gate * (1.0 + wide * (1.0 - gate))
        given = jnp.where(used[j], raw[j], none).astype(F32)
        value = given + slope * back_two[j]
        value = jnp.where(used[j], value, 0.0).astype(BF16)
        grad_mid[OWN, 1 + j] = value
        end_mid = value if j == 0 else jnp.where(filled == j + 1, value, end_mid)
    last[2] = end_mid
    grad_mid_copies = exchange(grad_mid, grad_mid_edge, last.at[2])
    for j in range(CAP):
        wide = first[j].astype(F32)
        act = (wide * jax.nn.sigmoid(wide)).astype(BF16)
        act_two[OWN, 1 + j] = act
        end_two = act if j == 0 else jnp.where(filled == j + 1, act, end_two)
        wide = blended[j].astype(F32)
        gate = jax.nn.sigmoid(wide)
        slope_one[j] = gate * (1.0 + wide * (1.0 - gate))
        low[j] = grad_mid[OWN, 1 + j].astype(F32)
    last[3] = end_two
    act_two_copies = exchange(act_two, act_two_edge, last.at[3])

    convolve(grad_mid_copies, grad_mid, grad_mid_edge, w_one, True)
    for j in range(CAP):
        low[j] += slope_one[j] * joined(j)

    def gathered(f):
        summed = mix[0, f] * low[0]
        for j in range(1, CAP):
            summed += mix[j, f] * low[j]
        return summed

    spread_copies = []
    for start, count, at, by in ((0, 2, 8, -2), (14, 2, 10, 2), (2, 4, 0, -1), (10, 4, 4, 1)):
        for f in range(start, start + count):
            spread[f] = gathered(f).astype(BF16)
        spread_copies.append(push(spread.at[pl.ds(start, count)], arrived.at[pl.ds(at, count)], by, r))
    for f in range(FRAMES):
        source_grad[f] = gathered(BELOW + f)

    convolve(act_two_copies, act_two, act_two_edge, w_two, False)
    for j in range(CAP):
        value = first[j].astype(F32) + joined(j) + b_two[...]
        decoded[j] = jnp.where(used[j], value, 0.0).astype(BF16)

    landed(*spread_copies)
    for f in range(FRAMES):
        value = source_grad[f]
        value += jnp.where(exists(1), arrived[f].astype(F32), 0.0)
        value += jnp.where(exists(-1), arrived[4 + f].astype(F32), 0.0)
        if f >= 2:
            value += jnp.where(exists(2), arrived[8 + f - 2].astype(F32), 0.0)
        else:
            value += jnp.where(exists(-2), arrived[10 + f].astype(F32), 0.0)
        source_grad[f] = value
    left(*copies)


def finish(decoded_in, grad_in, decoded, source_grad, done):
    one = pltpu.make_async_copy(decoded_in, decoded, done.at[0])
    two = pltpu.make_async_copy(grad_in, source_grad, done.at[1])
    one.start()
    two.start()
    one.wait()
    two.wait()


def solution(mesh):
    spans, lines = mesh.shape["tm"], mesh.shape["rows"]

    def body(
        source,
        frame_counts,
        tap_frames,
        tap_weights,
        kernel_one,
        bias_one,
        kernel_two,
        bias_two,
        upstream,
    ):
        box = pltpu.VMEM((3, CAP + 2, W, C), BF16)
        edge = pltpu.VMEM((3, W, C), BF16)
        slots = pltpu.VMEM((CAP, W, C), BF16)
        wide_slots = pltpu.VMEM((CAP, W, C), F32)
        kernels = pltpu.VMEM((3, 3, 3, C, C), BF16)
        bias = pltpu.VMEM((1, C), F32)
        decoded, source_grad = pl.pallas_call(
            lambda *refs: kernel(spans, lines, *refs),
            out_shape=(
                pltpu.VMEM((CAP, W, C), BF16),
                pltpu.VMEM((FRAMES, W, C), F32),
            ),
            in_specs=[pl.BlockSpec(memory_space=pl.ANY)] * 9,
            out_specs=[pl.BlockSpec(memory_space=pltpu.VMEM)] * 2,
            scratch_shapes=[
                pltpu.VMEM((WINDOW, W, C), BF16),
                kernels,
                kernels,
                bias,
                bias,
                slots,
                slots,
                slots,
                wide_slots,
                wide_slots,
                wide_slots,
                pltpu.VMEM((3, CAP * W, C), F32),
                box,
                box,
                box,
                box,
                edge,
                edge,
                edge,
                edge,
                pltpu.VMEM((4, W, C), BF16),
                pltpu.VMEM((WINDOW, W, C), BF16),
                pltpu.VMEM((12, W, C), BF16),
                pltpu.SMEM((CAP, WINDOW), F32),
                pltpu.SMEM((1,), jnp.int32),
                pltpu.SMEM((TAPS, CAP), jnp.int32),
                pltpu.SMEM((TAPS, CAP), F32),
                pltpu.SemaphoreType.DMA((9,)),
                pltpu.SemaphoreType.DMA((40,)),
                pltpu.SemaphoreType.DMA((40,)),
            ],
            compiler_params=pltpu.CompilerParams(
                collective_id=0, has_side_effects=True, vmem_limit_bytes=48 * 1024 * 1024
            ),
            cost_estimate=pl.CostEstimate(
                flops=4 * 2 * CAP * W * 27 * C * C,
                bytes_accessed=2 * 27 * C * C * 2,
                transcendentals=0,
            ),
        )(
            *(
                x if x is frame_counts else pltpu.with_memory_space_constraint(x, pltpu.HBM)
                for x in (
                    source.reshape(FRAMES, W, C),
                    frame_counts,
                    tap_frames.T,
                    tap_weights.T,
                    kernel_one,
                    bias_one.reshape(1, C),
                    kernel_two,
                    bias_two.reshape(1, C),
                    upstream.reshape(CAP, W, C),
                )
            )
        )
        decoded, source_grad = pl.pallas_call(
            finish,
            out_shape=(
                jax.ShapeDtypeStruct((CAP, W, C), BF16),
                jax.ShapeDtypeStruct((FRAMES, W, C), F32),
            ),
            in_specs=[pl.BlockSpec(memory_space=pltpu.VMEM)] * 2,
            out_specs=[pl.BlockSpec(memory_space=pl.ANY)] * 2,
            scratch_shapes=[pltpu.SemaphoreType.DMA((2,))],
        )(decoded, source_grad)
        return decoded.reshape(CAP, 1, W, C), source_grad.reshape(FRAMES, 1, W, C)

    whole = P("tm", "rows", None, None)
    return jax.shard_map(
        body,
        mesh=mesh,
        in_specs=(whole, P("tm"), P("tm", None), P("tm", None), P(), P(), P(), P(), whole),
        out_specs=(whole, whole),
        check_vma=False,
    )
```

time: 46.4 us -> 34.8 us (0.75)
  the two profiles are of different devices: /device:TPU:1 before, /device:TPU:122 now
where the time goes in v2:
time: 34.8 us; the launch traced here: 34.6 us
  Pallas kernels  32 us (92%)
  local copies, waits for them, and re-layouts  1.3 us (4%)
  between operations  1.3 us (4%)
    pallas_call x1, Pallas kernels, body(): pl.pallas_call(lambda *refs: kernel(spans, lines, *refs), out_shape=(pltp...  30.3 us
    pallas_call x1, Pallas kernels, body(): pl.pallas_call(finish, out_shape=(jax.ShapeDtypeStruct((CAP, W, C), BF16)...  1.69 us
    unnamed x4, local copies, waits for them, and re-layouts  1.3 us

profile of v2, /device:TPU:122, one launch (start us, length us, event | category | flops | bytes accessed | tf_op | source)
XLA Modules:
  0.0 34.6 jit_solution(14422088499363992437)
XLA Ops:
  1.3 30.3 %shard_map.104 = (bf16[9,32,256]{2,1,0:T(8,128)(2,1)S(1)}, f32[4,32,256]{2,1,0:T(8,128)S(1)}) custom-call(bf16[4,32,256]{2,1,0:T(8,128)(2,1)} %bitcast.15, s32[1]{0:T(128)S(6)} %copy.13.refs_1_, s32[4,9]{1,0:T(4,128)} %bitcast.16, f32[4,9]{1,0:T(4,128)} %bitcast.17, bf16[3,3,3,256,256]{4,3,2,1,0:T(8,128)(2,1)} %refs_4_.1, f32[1,256]{1,0:T(1,128)} %bitcast.18, ...), custom_call_target="tpu_custom_call" | custom-call | flops 4076863488 | bytes 7077888 | tf_op jit(solution)/shard_map/pallas_call | solution.py:365
  31.6 0.0 copy-start
  31.6 0.6 %copy-done = bf16[9,32,256]{2,1,0:T(8,128)(2,1)} copy-done((bf16[9,32,256]{2,1,0:T(8,128)(2,1)}, bf16[9,32,256]{2,1,0:T(8,128)(2,1)S(1)}, u32[]{:S(2)}) %copy-start) | copy-done | bytes 147480
  32.2 0.0 copy-start.1
  32.3 0.6 %copy-done.1 = f32[4,32,256]{2,1,0:T(8,128)} copy-done((f32[4,32,256]{2,1,0:T(8,128)}, f32[4,32,256]{2,1,0:T(8,128)S(1)}, u32[]{:S(2)}) %copy-start.1) | copy-done | bytes 131096
  32.9 1.7 %shard_map.105 = (bf16[9,32,256]{2,1,0:T(8,128)(2,1)}, f32[4,32,256]{2,1,0:T(8,128)}) custom-call(bf16[9,32,256]{2,1,0:T(8,128)(2,1)} %copy-done, f32[4,32,256]{2,1,0:T(8,128)} %copy-done.1), custom_call_target="tpu_custom_call" | custom-call | tf_op jit(solution)/shard_map/pallas_call | solution.py:429
Async XLA Ops:
  31.6 0.7 %copy-start = (bf16[9,32,256]{2,1,0:T(8,128)(2,1)}, bf16[9,32,256]{2,1,0:T(8,128)(2,1)S(1)}, u32[]{:S(2)}) copy-start(bf16[9,32,256]{2,1,0:T(8,128)(2,1)S(1)} %get-tuple-element.6.decoded_in) | copy-start | bytes 442372
  32.2 0.6 %copy-start.1 = (f32[4,32,256]{2,1,0:T(8,128)}, f32[4,32,256]{2,1,0:T(8,128)S(1)}, u32[]{:S(2)}) copy-start(f32[4,32,256]{2,1,0:T(8,128)S(1)} %get-tuple-element.7.grad_in) | copy-start | bytes 393220

commit v3 on v2

--- a/solution.py
+++ b/solution.py
@@ -44,6 +44,7 @@
     back_two,
     slope_one,
     parts,
+    after,
     inc,
     act_one,
     grad_mid,
@@ -157,21 +158,12 @@
     def exchange(box, edge, ends):
         mine = box.at[OWN, pl.ds(1, CAP)]
         head = box.at[OWN, 1]
-        far_last = push(ends, box.at[FAR, 0], 1, far)
-        far_head = push(head, edge.at[FAR], -1, far)
-        own_last = push(ends, box.at[OWN, 0], 1, r)
-        own_head = push(head, edge.at[OWN], -1, r)
+        far_edges = push(ends, edge.at[0, FAR], 1, far), push(head, edge.at[1, FAR], -1, far)
+        own_edges = push(ends, edge.at[0, OWN], 1, r), push(head, edge.at[1, OWN], -1, r)
+        near_edges = push(ends, edge.at[0, NEAR], 1, near), push(head, edge.at[1, NEAR], -1, near)
         far_mine = push(mine, box.at[FAR, pl.ds(1, CAP)], 0, far)
-        near_last = push(ends, box.at[NEAR, 0], 1, near)
-        near_head = push(head, edge.at[NEAR], -1, near)
         near_mine = push(mine, box.at[NEAR, pl.ds(1, CAP)], 0, near)
-        out = (far_head, own_head, near_head, far_mine, near_mine)
-        return (
-            (own_last, own_head),
-            (near_last, near_head, near_mine),
-            (far_last, far_head, far_mine),
-            out,
-        )
+        return (None, near_mine, far_mine), (own_edges, near_edges, far_edges)
 
     get_source.wait()
     pl.semaphore_wait(barrier, greeted)
@@ -188,6 +180,10 @@
     used = [j < filled for j in range(CAP)]
     none = jnp.zeros((W, C), BF16)
 
+    for box in (inc, act_one, grad_mid, act_two):
+        for s in (OWN, NEAR, FAR):
+            box[s, 0] = none
+            box[s, CAP + 1] = none
     get_raw.wait()
     for j in range(CAP):
         inc[OWN, 1 + j] = jnp.where(used[j], raw[j], none)
@@ -218,61 +214,80 @@
                 weight += jnp.where(f_s[k, j] == lowest + f, w_s[k, j], 0.0)
             mix[j, f] = jnp.where(used[j], weight, 0.0)
 
-    def settle(s, box, edge):
-        there = far_there if s == FAR else None
-        before = both(exists(-1), there)
-        after = both(exists(1), there)
-        box[s, 0] = jnp.where(before, box[s, 0], none)
-        follow = jnp.where(after, edge[s], none)
-        if s == FAR:
-            box[s, 1] = jnp.where(there, box[s, 1], none)
-        for e in range(2, CAP + 2):
-            held = box[s, e] if e <= CAP else none
-            if s == FAR:
-                held = jnp.where(there, held, none)
-            box[s, e] = jnp.where(filled + 1 == e, follow, held)
-
-    def convolve(copied, box, edge, w, back):
-        taps = (1, near_tap, far_tap)
-        left(*copied[3])
-        for s in (OWN, NEAR, FAR):
-            landed(*copied[s])
-            settle(s, box, edge)
+    def products(fields, w, s, back, c, depths):
+        tap = (1, near_tap, far_tap)[s]
+        if back:
+            tile = jnp.concatenate([w[2 - a, 2 - tap, 2 - c] for a in depths], axis=1)
+            dims = (((1,), (1,)), ((), ()))
+        else:
+            tile = jnp.concatenate([w[a, tap, c] for a in depths], axis=0)
+            dims = (((1,), (0,)), ((), ()))
+        return lax.dot_general(fields, tile, dims, preferred_element_type=F32)
+
+    def inner(copied, box, w, back, s):
+        def step():
+            if s != OWN:
+                copied[0][s][0].wait_recv()
             fields = jnp.concatenate(
                 [box[s, a : a + CAP].reshape(CAP * W, C) for a in range(3)], axis=1
             )
             for c in range(3):
-                if back:
-                    tile = jnp.concatenate([w[2 - a, 2 - taps[s], 2 - c] for a in range(3)], axis=1)
-                    dims = (((1,), (1,)), ((), ()))
-                else:
-                    tile = jnp.concatenate([w[a, taps[s], c] for a in range(3)], axis=0)
-                    dims = (((1,), (0,)), ((), ()))
-                term = lax.dot_general(fields, tile, dims, preferred_element_type=F32)
+                term = products(fields, w, s, back, c, (0, 1, 2))
                 if s == OWN:
                     parts[c] = term
                 else:
                     parts[c] += term
 
+        when(far_there if s == FAR else None, step)
+        if s != OWN:
+            copied[0][s][4] = False
+
+    def border(copied, edge, w, back, s):
+        landed(*copied[1][s])
+        there = far_there if s == FAR else None
+        first_edge = jnp.where(both(exists(-1), there), edge[0, s], none)
+        after_edge = jnp.where(both(exists(1), there), edge[1, s], none)
+        for c in range(3):
+            parts[c, :W] += products(first_edge, w, s, back, c, (0,))
+            term = products(after_edge, w, s, back, c, (2,))
+            if s == OWN:
+                after[c] = term
+            else:
+                after[c] += term
+
     column = lax.broadcasted_iota(jnp.int32, (W, C), 0)
 
-    def joined(j):
-        rows = pl.ds(j * W, W)
-        before = jnp.where(column == 0, 0.0, pltpu.roll(parts[0, rows], 1, 0))
-        after = jnp.where(column == W - 1, 0.0, pltpu.roll(parts[2, rows], W - 1, 0))
-        return parts[1, rows] + before + after
+    def shifted(lower, centre, upper):
+        lower = jnp.where(column == 0, 0.0, pltpu.roll(lower, 1, 0))
+        upper = jnp.where(column == W - 1, 0.0, pltpu.roll(upper, W - 1, 0))
+        return lower + centre + upper
+
+    def joined():
+        extra = shifted(after[0], after[1], after[2])
+        for j in range(CAP):
+            rows = pl.ds(j * W, W)
+            value = shifted(parts[0, rows], parts[1, rows], parts[2, rows])
+            yield j, value + jnp.where(filled == j + 1, extra, 0.0)
+
+    def convolve(copied, box, edge, w, back):
+        inner(copied, box, w, back, OWN)
+        inner(copied, box, w, back, NEAR)
+        border(copied, edge, w, back, OWN)
+        border(copied, edge, w, back, NEAR)
+        inner(copied, box, w, back, FAR)
+        border(copied, edge, w, back, FAR)
 
     get_two.wait()
     convolve(inc_copies, inc, inc_edge, w_two, True)
-    for j in range(CAP):
-        back_two[j] = joined(j)
+    for j, value in joined():
+        back_two[j] = value
 
     get_one.wait()
     get_b_one.wait()
     get_b_two.wait()
     convolve(act_one_copies, act_one, act_one_edge, w_one, False)
-    for j in range(CAP):
-        value = blended[j].astype(F32) + joined(j) + b_one[...]
+    for j, value in joined():
+        value += blended[j].astype(F32) + b_one[...]
         value = jnp.where(used[j], value, 0.0).astype(BF16)
         first[j] = value
         wide = value.astype(F32)
@@ -298,8 +313,8 @@
     act_two_copies = exchange(act_two, act_two_edge, last.at[3])
 
     convolve(grad_mid_copies, grad_mid, grad_mid_edge, w_one, True)
-    for j in range(CAP):
-        low[j] += slope_one[j] * joined(j)
+    for j, value in joined():
+        low[j] += slope_one[j] * value
 
     def gathered(f):
         summed = mix[0, f] * low[0]
@@ -316,8 +331,8 @@
         source_grad[f] = gathered(BELOW + f)
 
     convolve(act_two_copies, act_two, act_two_edge, w_two, False)
-    for j in range(CAP):
-        value = first[j].astype(F32) + joined(j) + b_two[...]
+    for j, value in joined():
+        value += first[j].astype(F32) + b_two[...]
         decoded[j] = jnp.where(used[j], value, 0.0).astype(BF16)
 
     landed(*spread_copies)
@@ -357,7 +372,7 @@
         upstream,
     ):
         box = pltpu.VMEM((3, CAP + 2, W, C), BF16)
-        edge = pltpu.VMEM((3, W, C), BF16)
+        edge = pltpu.VMEM((2, 3, W, C), BF16)
         slots = pltpu.VMEM((CAP, W, C), BF16)
         wide_slots = pltpu.VMEM((CAP, W, C), F32)
         kernels = pltpu.VMEM((3, 3, 3, C, C), BF16)
@@ -383,6 +398,7 @@
                 wide_slots,
                 wide_slots,
                 pltpu.VMEM((3, CAP * W, C), F32),
+                pltpu.VMEM((3, W, C), F32),
                 box,
                 box,
                 box,
@@ -435,7 +451,7 @@
             in_specs=[pl.BlockSpec(memory_space=pltpu.VMEM)] * 2,
             out_specs=[pl.BlockSpec(memory_space=pl.ANY)] * 2,
             scratch_shapes=[pltpu.SemaphoreType.DMA((2,))],
-        )(decoded, source_grad)
+        )(*(pltpu.with_memory_space_constraint(x, pltpu.VMEM) for x in (decoded, source_grad)))
         return decoded.reshape(CAP, 1, W, C), source_grad.reshape(FRAMES, 1, W, C)
 
     whole = P("tm", "rows", None, None)

time: 34.8 us -> 31.3 us (0.90)
  Pallas kernels: 32 us -> 29.9 us
  local copies, waits for them, and re-layouts: 1.3 us -> 0 us
    unnamed x4 -> x0, local copies, waits for them, and re-layouts: 1.3 us -> none
    pallas_call x1, Pallas kernels: 30.3 us -> 29.1 us  [body(): pl.pallas_call(lambda *refs: kernel(spans, lines, *refs), out_shape=(pltp...]
    pallas_call x1, Pallas kernels: 1.69 us -> 0.72 us  [body(): pl.pallas_call(finish, out_shape=(jax.ShapeDtypeStruct((CAP, W, C), BF16)...]
where the time goes in v3:
time: 31.3 us; the launch traced here: 31.2 us
  Pallas kernels  29.9 us (96%)
  between operations  1.29 us (4%)
    pallas_call x1, Pallas kernels, body(): pl.pallas_call(lambda *refs: kernel(spans, lines, *refs), out_shape=(pltp...  29.1 us
    pallas_call x1, Pallas kernels, body(): pl.pallas_call(finish, out_shape=(jax.ShapeDtypeStruct((CAP, W, C), BF16)...  0.72 us

profile of v3, /device:TPU:122, one launch (start us, length us, event | category | flops | bytes accessed | tf_op | source)
XLA Modules:
  0.0 31.2 jit_solution(12088580358656366509)
XLA Ops:
  1.3 29.1 %shard_map.104 = (bf16[9,32,256]{2,1,0:T(8,128)(2,1)S(1)}, f32[4,32,256]{2,1,0:T(8,128)S(1)}) custom-call(bf16[4,32,256]{2,1,0:T(8,128)(2,1)} %bitcast.15, s32[1]{0:T(128)S(6)} %copy.13.refs_1_, s32[4,9]{1,0:T(4,128)} %bitcast.16, f32[4,9]{1,0:T(4,128)} %bitcast.17, bf16[3,3,3,256,256]{4,3,2,1,0:T(8,128)(2,1)} %refs_4_.1, f32[1,256]{1,0:T(1,128)} %bitcast.18, ...), custom_call_target="tpu_custom_call" | custom-call | flops 4076863488 | bytes 7077888 | tf_op jit(solution)/shard_map/pallas_call | solution.py:380
  30.4 0.7 %shard_map.105 = (bf16[9,32,256]{2,1,0:T(8,128)(2,1)}, f32[4,32,256]{2,1,0:T(8,128)}) custom-call(bf16[9,32,256]{2,1,0:T(8,128)(2,1)S(1)} %get-tuple-element.6.decoded_in, f32[4,32,256]{2,1,0:T(8,128)S(1)} %get-tuple-element.7.grad_in), custom_call_target="tpu_custom_call" | custom-call | tf_op jit(solution)/shard_map/pallas_call | solution.py:445

commit v4 on v3

--- a/solution.py
+++ b/solution.py
@@ -95,7 +95,6 @@
         return far_there if row is far else None
 
     reach = [(by, r) for by in (-2, -1, 1, 2)] + [(0, near), (0, far)]
-    reach += [(by, row) for by in (-1, 1) for row in (near, far)]
     barrier = pltpu.get_barrier_semaphore()
     greeted = jnp.int32(0)
     for by, row in reach:
@@ -128,7 +127,7 @@
 
     copies = []
 
-    def push(src, dst, by, row):
+    def push(src, dst, by, row, held=None):
         k = len(copies)
         copy = pltpu.make_async_remote_copy(
             src_ref=src,
@@ -138,8 +137,9 @@
             device_id={"tm": d + by, "rows": row},
             device_id_type=MESH,
         )
-        when(both(exists(by), line(row)), copy.start)
-        entry = [copy, both(exists(by), line(row)), both(exists(-by), line(row)), True, True]
+        sent = both(both(exists(by), line(row)), held)
+        when(sent, copy.start)
+        entry = [copy, sent, both(both(exists(-by), line(row)), held), True, True]
         copies.append(entry)
         return entry
 
@@ -155,15 +155,18 @@
                 when(entry[1], entry[0].wait_send)
                 entry[3] = False
 
-    def exchange(box, edge, ends):
-        mine = box.at[OWN, pl.ds(1, CAP)]
+    def send_edges(box, edge, ends):
         head = box.at[OWN, 1]
         far_edges = push(ends, edge.at[0, FAR], 1, far), push(head, edge.at[1, FAR], -1, far)
         own_edges = push(ends, edge.at[0, OWN], 1, r), push(head, edge.at[1, OWN], -1, r)
         near_edges = push(ends, edge.at[0, NEAR], 1, near), push(head, edge.at[1, NEAR], -1, near)
+        return own_edges, near_edges, far_edges
+
+    def send_slots(box):
+        mine = box.at[OWN, pl.ds(1, CAP)]
         far_mine = push(mine, box.at[FAR, pl.ds(1, CAP)], 0, far)
         near_mine = push(mine, box.at[NEAR, pl.ds(1, CAP)], 0, near)
-        return (None, near_mine, far_mine), (own_edges, near_edges, far_edges)
+        return None, near_mine, far_mine
 
     get_source.wait()
     pl.semaphore_wait(barrier, greeted)
@@ -187,32 +190,48 @@
     get_raw.wait()
     for j in range(CAP):
         inc[OWN, 1 + j] = jnp.where(used[j], raw[j], none)
-    last[0] = raw[jnp.clip(filled - 1, 0, CAP - 1)]
-    inc_copies = exchange(inc, inc_edge, last.at[0])
-
+
+    end = jnp.clip(filled - 1, 0, CAP - 1)
+    last[0] = raw[end]
+    inc_slots = send_slots(inc)
+    edges = (
+        push(last.at[0], inc_edge.at[0, OWN], 1, r),
+        push(inc.at[OWN, 1], inc_edge.at[1, OWN], -1, r),
+    )
+    inc_edges = [edges]
     get_frames.wait()
     get_weights.wait()
+    landed(*edges)
+    for s, row in ((NEAR, near), (FAR, far)):
+        inc_edges.append(
+            [
+                push(inc_edge.at[k, OWN], inc_edge.at[k, s], 0, row, exists((-1, 1)[k]))
+                for k in range(2)
+            ]
+        )
     landed(*sources)
-    for j in range(CAP):
+
+    def blend(j):
         summed = jnp.zeros((W, C), F32)
         for k in range(TAPS):
             at = jnp.clip(f_s[k, j] - lowest, 0, WINDOW - 1)
             summed += w_s[k, j] * window[at].astype(F32)
-        value = jnp.where(used[j], summed, 0.0).astype(BF16)
+        return summed.astype(BF16)
+
+    def silu(value):
+        wide = value.astype(F32)
+        return (wide * jax.nn.sigmoid(wide)).astype(BF16)
+
+    value = blend(0)
+    blended[0] = value
+    act_one[OWN, 1] = silu(value)
+    last[1] = silu(blend(end))
+    act_one_edges = send_edges(act_one, act_one_edge, last.at[1])
+    for j in range(1, CAP):
+        value = jnp.where(used[j], blend(j), none)
         blended[j] = value
-        wide = value.astype(F32)
-        value = (wide * jax.nn.sigmoid(wide)).astype(BF16)
-        act_one[OWN, 1 + j] = value
-        end = value if j == 0 else jnp.where(filled == j + 1, value, end)
-    last[1] = end
-    act_one_copies = exchange(act_one, act_one_edge, last.at[1])
-
-    for j in range(CAP):
-        for f in range(WINDOW):
-            weight = jnp.float32(0.0)
-            for k in range(TAPS):
-                weight += jnp.where(f_s[k, j] == lowest + f, w_s[k, j], 0.0)
-            mix[j, f] = jnp.where(used[j], weight, 0.0)
+        act_one[OWN, 1 + j] = silu(value)
+    act_one_slots = send_slots(act_one)
 
     def products(fields, w, s, back, c, depths):
         tap = (1, near_tap, far_tap)[s]
@@ -224,31 +243,31 @@
             dims = (((1,), (0,)), ((), ()))
         return lax.dot_general(fields, tile, dims, preferred_element_type=F32)
 
-    def inner(copied, box, w, back, s):
+    def inner(slots, box, w, back, s):
         def step():
             if s != OWN:
-                copied[0][s][0].wait_recv()
+                slots[s][0].wait_recv()
             fields = jnp.concatenate(
                 [box[s, a : a + CAP].reshape(CAP * W, C) for a in range(3)], axis=1
             )
             for c in range(3):
                 term = products(fields, w, s, back, c, (0, 1, 2))
                 if s == OWN:
-                    parts[c] = term
+                    parts[c] = term.reshape(CAP, W, C)
                 else:
-                    parts[c] += term
+                    parts[c] += term.reshape(CAP, W, C)
 
         when(far_there if s == FAR else None, step)
         if s != OWN:
-            copied[0][s][4] = False
-
-    def border(copied, edge, w, back, s):
-        landed(*copied[1][s])
+            slots[s][4] = False
+
+    def border(edges, edge, w, back, s):
+        landed(*edges[s])
         there = far_there if s == FAR else None
         first_edge = jnp.where(both(exists(-1), there), edge[0, s], none)
         after_edge = jnp.where(both(exists(1), there), edge[1, s], none)
         for c in range(3):
-            parts[c, :W] += products(first_edge, w, s, back, c, (0,))
+            parts[c, 0] += products(first_edge, w, s, back, c, (0,))
             term = products(after_edge, w, s, back, c, (2,))
             if s == OWN:
                 after[c] = term
@@ -262,59 +281,67 @@
         upper = jnp.where(column == W - 1, 0.0, pltpu.roll(upper, W - 1, 0))
         return lower + centre + upper
 
-    def joined():
-        extra = shifted(after[0], after[1], after[2])
-        for j in range(CAP):
-            rows = pl.ds(j * W, W)
-            value = shifted(parts[0, rows], parts[1, rows], parts[2, rows])
-            yield j, value + jnp.where(filled == j + 1, extra, 0.0)
-
-    def convolve(copied, box, edge, w, back):
-        inner(copied, box, w, back, OWN)
-        inner(copied, box, w, back, NEAR)
-        border(copied, edge, w, back, OWN)
-        border(copied, edge, w, back, NEAR)
-        inner(copied, box, w, back, FAR)
-        border(copied, edge, w, back, FAR)
+    def slot(j):
+        return shifted(parts[0, j], parts[1, j], parts[2, j])
+
+    def joined(extra, j):
+        return slot(j) + jnp.where(filled == j + 1, extra, 0.0)
+
+    def convolve(slots, edges, box, edge, w, back):
+        for s in (OWN, NEAR, FAR):
+            inner(slots, box, w, back, s)
+        for s in (OWN, NEAR, FAR):
+            border(edges, edge, w, back, s)
+        return shifted(after[0], after[1], after[2])
 
     get_two.wait()
-    convolve(inc_copies, inc, inc_edge, w_two, True)
-    for j, value in joined():
-        back_two[j] = value
+    extra = convolve(inc_slots, inc_edges, inc, inc_edge, w_two, True)
+    for j in range(CAP):
+        back_two[j] = joined(extra, j)
 
     get_one.wait()
     get_b_one.wait()
     get_b_two.wait()
-    convolve(act_one_copies, act_one, act_one_edge, w_one, False)
-    for j, value in joined():
-        value += blended[j].astype(F32) + b_one[...]
-        value = jnp.where(used[j], value, 0.0).astype(BF16)
-        first[j] = value
+    extra = convolve(act_one_slots, act_one_edges, act_one, act_one_edge, w_one, False)
+
+    def first_at(j, conv):
+        return (conv + blended[j].astype(F32) + b_one[...]).astype(BF16)
+
+    def grad_at(j, value):
         wide = value.astype(F32)
         gate = jax.nn.sigmoid(wide)
         slope = gate * (1.0 + wide * (1.0 - gate))
-        given = jnp.where(used[j], raw[j], none).astype(F32)
-        value = given + slope * back_two[j]
-        value = jnp.where(used[j], value, 0.0).astype(BF16)
-        grad_mid[OWN, 1 + j] = value
-        end_mid = value if j == 0 else jnp.where(filled == j + 1, value, end_mid)
-    last[2] = end_mid
-    grad_mid_copies = exchange(grad_mid, grad_mid_edge, last.at[2])
-    for j in range(CAP):
-        wide = first[j].astype(F32)
-        act = (wide * jax.nn.sigmoid(wide)).astype(BF16)
-        act_two[OWN, 1 + j] = act
-        end_two = act if j == 0 else jnp.where(filled == j + 1, act, end_two)
+        return (raw[j].astype(F32) + slope * back_two[j]).astype(BF16)
+
+    value = first_at(0, joined(extra, 0))
+    first[0] = value
+    grad_mid[OWN, 1] = grad_at(0, value)
+    value = first_at(end, slot(end) + extra)
+    last[2] = grad_at(end, value)
+    grad_mid_edges = send_edges(grad_mid, grad_mid_edge, last.at[2])
+    last[3] = silu(value)
+    for j in range(1, CAP):
+        value = jnp.where(used[j], first_at(j, joined(extra, j)), none)
+        first[j] = value
+        grad_mid[OWN, 1 + j] = jnp.where(used[j], grad_at(j, value), none)
+    grad_mid_slots = send_slots(grad_mid)
+    for j in range(CAP):
+        act_two[OWN, 1 + j] = silu(first[j])
+    act_two_edges = send_edges(act_two, act_two_edge, last.at[3])
+    act_two_slots = send_slots(act_two)
+    for j in range(CAP):
         wide = blended[j].astype(F32)
         gate = jax.nn.sigmoid(wide)
         slope_one[j] = gate * (1.0 + wide * (1.0 - gate))
-        low[j] = grad_mid[OWN, 1 + j].astype(F32)
-    last[3] = end_two
-    act_two_copies = exchange(act_two, act_two_edge, last.at[3])
-
-    convolve(grad_mid_copies, grad_mid, grad_mid_edge, w_one, True)
-    for j, value in joined():
-        low[j] += slope_one[j] * value
+        for f in range(WINDOW):
+            weight = jnp.float32(0.0)
+            for k in range(TAPS):
+                weight += jnp.where(f_s[k, j] == lowest + f, w_s[k, j], 0.0)
+            mix[j, f] = jnp.where(used[j], weight, 0.0)
+
+    extra = convolve(grad_mid_slots, grad_mid_edges, grad_mid, grad_mid_edge, w_one, True)
+    for j in range(CAP):
+        low[j] = grad_mid[OWN, 1 + j].astype(F32) + slope_one[j] * joined(extra, j)
 
     def gathered(f):
         summed = mix[0, f] * low[0]
@@ -330,9 +357,9 @@
     for f in range(FRAMES):
         source_grad[f] = gathered(BELOW + f)
 
-    convolve(act_two_copies, act_two, act_two_edge, w_two, False)
-    for j, value in joined():
-        value += first[j].astype(F32) + b_two[...]
+    extra = convolve(act_two_slots, act_two_edges, act_two, act_two_edge, w_two, False)
+    for j in range(CAP):
+        value = joined(extra, j) + first[j].astype(F32) + b_two[...]
         decoded[j] = jnp.where(used[j], value, 0.0).astype(BF16)
 
     landed(*spread_copies)
@@ -397,7 +424,7 @@
                 wide_slots,
                 wide_slots,
                 wide_slots,
-                pltpu.VMEM((3, CAP * W, C), F32),
+                pltpu.VMEM((3, CAP, W, C), F32),
                 pltpu.VMEM((3, W, C), F32),
                 box,
                 box,

time: 31.3 us -> 29.8 us (0.952)
  Pallas kernels: 29.9 us -> 28.3 us
    pallas_call x1, Pallas kernels: 29.1 us -> 27.6 us  [body(): pl.pallas_call(lambda *refs: kernel(spans, lines, *refs), out_shape=(pltp...]
where the time goes in v4:
time: 29.8 us; the launch traced here: 29.6 us
  Pallas kernels  28.3 us (95%)
  between operations  1.29 us (4%)
    pallas_call x1, Pallas kernels, body(): pl.pallas_call(lambda *refs: kernel(spans, lines, *refs), out_shape=(pltp...  27.6 us
    pallas_call x1, Pallas kernels, body(): pl.pallas_call(finish, out_shape=(jax.ShapeDtypeStruct((CAP, W, C), BF16)...  0.72 us

profile of v4, /device:TPU:122, one launch (start us, length us, event | category | flops | bytes accessed | tf_op | source)
XLA Modules:
  0.0 29.6 jit_solution(3806199158753551618)
XLA Ops:
  1.3 27.6 %shard_map.104 = (bf16[9,32,256]{2,1,0:T(8,128)(2,1)S(1)}, f32[4,32,256]{2,1,0:T(8,128)S(1)}) custom-call(bf16[4,32,256]{2,1,0:T(8,128)(2,1)} %bitcast.15, s32[1]{0:T(128)S(6)} %copy.13.refs_1_, s32[4,9]{1,0:T(4,128)} %bitcast.16, f32[4,9]{1,0:T(4,128)} %bitcast.17, bf16[3,3,3,256,256]{4,3,2,1,0:T(8,128)(2,1)} %refs_4_.1, f32[1,256]{1,0:T(1,128)} %bitcast.18, ...), custom_call_target="tpu_custom_call" | custom-call | flops 4076863488 | bytes 7077888 | tf_op jit(solution)/shard_map/pallas_call | solution.py:407
  28.9 0.7 %shard_map.105 = (bf16[9,32,256]{2,1,0:T(8,128)(2,1)}, f32[4,32,256]{2,1,0:T(8,128)}) custom-call(bf16[9,32,256]{2,1,0:T(8,128)(2,1)S(1)} %get-tuple-element.6.decoded_in, f32[4,32,256]{2,1,0:T(8,128)S(1)} %get-tuple-element.7.grad_in), custom_call_target="tpu_custom_call" | custom-call | tf_op jit(solution)/shard_map/pallas_call | solution.py:472

commit v5 on v4

--- a/solution.py
+++ b/solution.py
@@ -201,38 +201,6 @@
     inc_edges = [edges]
     get_frames.wait()
     get_weights.wait()
-    landed(*edges)
-    for s, row in ((NEAR, near), (FAR, far)):
-        inc_edges.append(
-            [
-                push(inc_edge.at[k, OWN], inc_edge.at[k, s], 0, row, exists((-1, 1)[k]))
-                for k in range(2)
-            ]
-        )
-    landed(*sources)
-
-    def blend(j):
-        summed = jnp.zeros((W, C), F32)
-        for k in range(TAPS):
-            at = jnp.clip(f_s[k, j] - lowest, 0, WINDOW - 1)
-            summed += w_s[k, j] * window[at].astype(F32)
-        return summed.astype(BF16)
-
-    def silu(value):
-        wide = value.astype(F32)
-        return (wide * jax.nn.sigmoid(wide)).astype(BF16)
-
-    value = blend(0)
-    blended[0] = value
-    act_one[OWN, 1] = silu(value)
-    last[1] = silu(blend(end))
-    act_one_edges = send_edges(act_one, act_one_edge, last.at[1])
-    for j in range(1, CAP):
-        value = jnp.where(used[j], blend(j), none)
-        blended[j] = value
-        act_one[OWN, 1 + j] = silu(value)
-    act_one_slots = send_slots(act_one)
-
     def products(fields, w, s, back, c, depths):
         tap = (1, near_tap, far_tap)[s]
         if back:
@@ -287,15 +255,56 @@
     def joined(extra, j):
         return slot(j) + jnp.where(filled == j + 1, extra, 0.0)
 
-    def convolve(slots, edges, box, edge, w, back):
+    def inners(slots, box, w, back):
         for s in (OWN, NEAR, FAR):
             inner(slots, box, w, back, s)
+
+    def borders(edges, edge, w, back):
         for s in (OWN, NEAR, FAR):
             border(edges, edge, w, back, s)
         return shifted(after[0], after[1], after[2])
 
+    def convolve(slots, edges, box, edge, w, back):
+        inners(slots, box, w, back)
+        return borders(edges, edge, w, back)
+
     get_two.wait()
-    extra = convolve(inc_slots, inc_edges, inc, inc_edge, w_two, True)
+    inner(inc_slots, inc, w_two, True, OWN)
+    inner(inc_slots, inc, w_two, True, NEAR)
+    landed(*edges)
+    for s, row in ((NEAR, near), (FAR, far)):
+        inc_edges.append(
+            [
+                push(inc_edge.at[k, OWN], inc_edge.at[k, s], 0, row, exists((-1, 1)[k]))
+                for k in range(2)
+            ]
+        )
+    inner(inc_slots, inc, w_two, True, FAR)
+    landed(*sources)
+
+    def blend(j):
+        summed = jnp.zeros((W, C), F32)
+        for k in range(TAPS):
+            at = jnp.clip(f_s[k, j] - lowest, 0, WINDOW - 1)
+            summed += w_s[k, j] * window[at].astype(F32)
+        return summed.astype(BF16)
+
+    def silu(value):
+        wide = value.astype(F32)
+        return (wide * jax.nn.sigmoid(wide)).astype(BF16)
+
+    value = blend(0)
+    blended[0] = value
+    act_one[OWN, 1] = silu(value)
+    last[1] = silu(blend(end))
+    act_one_edges = send_edges(act_one, act_one_edge, last.at[1])
+    for j in range(1, CAP):
+        value = jnp.where(used[j], blend(j), none)
+        blended[j] = value
+        act_one[OWN, 1 + j] = silu(value)
+    act_one_slots = send_slots(act_one)
+
+    extra = borders(inc_edges, inc_edge, w_two, True)
     for j in range(CAP):
         back_two[j] = joined(extra, j)
 

time: 29.8 us -> 30.1 us (1.010)
  Pallas kernels: 28.3 us -> 28.7 us
    pallas_call x1, Pallas kernels: 27.6 us -> 28 us  [body(): pl.pallas_call(lambda *refs: kernel(spans, lines, *refs), out_shape=(pltp...]
where the time goes in v5:
time: 30.1 us; the launch traced here: 30 us
  Pallas kernels  28.7 us (95%)
  between operations  1.29 us (4%)
    pallas_call x1, Pallas kernels, body(): pl.pallas_call(lambda *refs: kernel(spans, lines, *refs), out_shape=(pltp...  28 us
    pallas_call x1, Pallas kernels, body(): pl.pallas_call(finish, out_shape=(jax.ShapeDtypeStruct((CAP, W, C), BF16)...  0.72 us

profile of v5, /device:TPU:122, one launch (start us, length us, event | category | flops | bytes accessed | tf_op | source)
XLA Modules:
  0.0 30.0 jit_solution(11679238811061206734)
XLA Ops:
  1.3 28.0 %shard_map.104 = (bf16[9,32,256]{2,1,0:T(8,128)(2,1)S(1)}, f32[4,32,256]{2,1,0:T(8,128)S(1)}) custom-call(bf16[4,32,256]{2,1,0:T(8,128)(2,1)} %bitcast.15, s32[1]{0:T(128)S(6)} %copy.13.refs_1_, s32[4,9]{1,0:T(4,128)} %bitcast.16, f32[4,9]{1,0:T(4,128)} %bitcast.17, bf16[3,3,3,256,256]{4,3,2,1,0:T(8,128)(2,1)} %refs_4_.1, f32[1,256]{1,0:T(1,128)} %bitcast.18, ...), custom_call_target="tpu_custom_call" | custom-call | flops 4076863488 | bytes 7077888 | tf_op jit(solution)/shard_map/pallas_call | solution.py:416
  29.3 0.7 %shard_map.105 = (bf16[9,32,256]{2,1,0:T(8,128)(2,1)}, f32[4,32,256]{2,1,0:T(8,128)}) custom-call(bf16[9,32,256]{2,1,0:T(8,128)(2,1)S(1)} %get-tuple-element.6.decoded_in, f32[4,32,256]{2,1,0:T(8,128)S(1)} %get-tuple-element.7.grad_in), custom_call_target="tpu_custom_call" | custom-call | tf_op jit(solution)/shard_map/pallas_call | solution.py:481

commit v6 on v5

--- a/solution.py
+++ b/solution.py
@@ -44,7 +44,9 @@
     back_two,
     slope_one,
     parts,
-    after,
+    fringe,
+    plain,
+    partial,
     inc,
     act_one,
     grad_mid,
@@ -235,12 +237,12 @@
         first_edge = jnp.where(both(exists(-1), there), edge[0, s], none)
         after_edge = jnp.where(both(exists(1), there), edge[1, s], none)
         for c in range(3):
-            parts[c, 0] += products(first_edge, w, s, back, c, (0,))
-            term = products(after_edge, w, s, back, c, (2,))
-            if s == OWN:
-                after[c] = term
-            else:
-                after[c] += term
+            for side, field, depth in ((0, first_edge, 0), (1, after_edge, 2)):
+                term = products(field, w, s, back, c, (depth,))
+                if s == OWN:
+                    fringe[side, c] = term
+                else:
+                    fringe[side, c] += term
 
     column = lax.broadcasted_iota(jnp.int32, (W, C), 0)
 
@@ -252,9 +254,6 @@
     def slot(j):
         return shifted(parts[0, j], parts[1, j], parts[2, j])
 
-    def joined(extra, j):
-        return slot(j) + jnp.where(filled == j + 1, extra, 0.0)
-
     def inners(slots, box, w, back):
         for s in (OWN, NEAR, FAR):
             inner(slots, box, w, back, s)
@@ -262,11 +261,21 @@
     def borders(edges, edge, w, back):
         for s in (OWN, NEAR, FAR):
             border(edges, edge, w, back, s)
-        return shifted(after[0], after[1], after[2])
-
-    def convolve(slots, edges, box, edge, w, back):
-        inners(slots, box, w, back)
-        return borders(edges, edge, w, back)
+        return (shifted(*(fringe[side, c] for c in range(3))) for side in range(2))
+
+    def patched(value, j, start, stop):
+        if j == 0:
+            value = value + start
+        return value + jnp.where(filled == j + 1, stop, 0.0)
+
+    for j in range(CAP):
+        tap_at = [f_s[k, j] - lowest for k in range(TAPS)]
+        tap_by = [jnp.where(used[j], w_s[k, j], 0.0) for k in range(TAPS)]
+        for f in range(WINDOW):
+            weight = jnp.float32(0.0)
+            for k in range(TAPS):
+                weight += jnp.where(tap_at[k] == f, tap_by[k], 0.0)
+            mix[j, f] = weight
 
     get_two.wait()
     inner(inc_slots, inc, w_two, True, OWN)
@@ -280,6 +289,8 @@
             ]
         )
     inner(inc_slots, inc, w_two, True, FAR)
+    for j in range(CAP):
+        back_two[j] = slot(j)
     landed(*sources)
 
     def blend(j):
@@ -304,71 +315,82 @@
         act_one[OWN, 1 + j] = silu(value)
     act_one_slots = send_slots(act_one)
 
-    extra = borders(inc_edges, inc_edge, w_two, True)
-    for j in range(CAP):
-        back_two[j] = joined(extra, j)
+    start, stop = borders(inc_edges, inc_edge, w_two, True)
+    for j in range(CAP):
+        back_two[j] = patched(back_two[j], j, start, stop)
+
+    def slope(value):
+        wide = value.astype(F32)
+        gate = jax.nn.sigmoid(wide)
+        return gate * (1.0 + wide * (1.0 - gate))
+
+    for j in range(CAP):
+        slope_one[j] = slope(blended[j])
+
+    def grad_at(j, value):
+        return (raw[j].astype(F32) + slope(value) * back_two[j]).astype(BF16)
 
     get_one.wait()
     get_b_one.wait()
     get_b_two.wait()
-    extra = convolve(act_one_slots, act_one_edges, act_one, act_one_edge, w_one, False)
-
-    def first_at(j, conv):
-        return (conv + blended[j].astype(F32) + b_one[...]).astype(BF16)
-
-    def grad_at(j, value):
-        wide = value.astype(F32)
-        gate = jax.nn.sigmoid(wide)
-        slope = gate * (1.0 + wide * (1.0 - gate))
-        return (raw[j].astype(F32) + slope * back_two[j]).astype(BF16)
-
-    value = first_at(0, joined(extra, 0))
+    inners(act_one_slots, act_one, w_one, False)
+    for j in range(CAP):
+        value = slot(j) + blended[j].astype(F32) + b_one[...]
+        plain[j] = value
+        if j > 0:
+            value = jnp.where(used[j], value.astype(BF16), none)
+            first[j] = value
+            grad_mid[OWN, 1 + j] = jnp.where(used[j], grad_at(j, value), none)
+            act_two[OWN, 1 + j] = silu(value)
+    start, stop = borders(act_one_edges, act_one_edge, w_one, False)
+    value = patched(plain[0], 0, start, stop).astype(BF16)
     first[0] = value
     grad_mid[OWN, 1] = grad_at(0, value)
-    value = first_at(end, slot(end) + extra)
-    last[2] = grad_at(end, value)
+    stop_first = (plain[end] + stop + jnp.where(end == 0, start, 0.0)).astype(BF16)
+    stop_grad = grad_at(end, stop_first)
+    last[2] = stop_grad
     grad_mid_edges = send_edges(grad_mid, grad_mid_edge, last.at[2])
-    last[3] = silu(value)
     for j in range(1, CAP):
-        value = jnp.where(used[j], first_at(j, joined(extra, j)), none)
-        first[j] = value
-        grad_mid[OWN, 1 + j] = jnp.where(used[j], grad_at(j, value), none)
+        at_end = filled == j + 1
+        grad_mid[OWN, 1 + j] = jnp.where(at_end, stop_grad, grad_mid[OWN, 1 + j])
     grad_mid_slots = send_slots(grad_mid)
-    for j in range(CAP):
-        act_two[OWN, 1 + j] = silu(first[j])
+    act_two[OWN, 1] = silu(value)
+    stop_act = silu(stop_first)
+    last[3] = stop_act
+    for j in range(1, CAP):
+        at_end = filled == j + 1
+        first[j] = jnp.where(at_end, stop_first, first[j])
+        act_two[OWN, 1 + j] = jnp.where(at_end, stop_act, act_two[OWN, 1 + j])
     act_two_edges = send_edges(act_two, act_two_edge, last.at[3])
     act_two_slots = send_slots(act_two)
-    for j in range(CAP):
-        wide = blended[j].astype(F32)
-        gate = jax.nn.sigmoid(wide)
-        slope_one[j] = gate * (1.0 + wide * (1.0 - gate))
-        for f in range(WINDOW):
-            weight = jnp.float32(0.0)
-            for k in range(TAPS):
-                weight += jnp.where(f_s[k, j] == lowest + f, w_s[k, j], 0.0)
-            mix[j, f] = jnp.where(used[j], weight, 0.0)
-
-    extra = convolve(grad_mid_slots, grad_mid_edges, grad_mid, grad_mid_edge, w_one, True)
-    for j in range(CAP):
-        low[j] = grad_mid[OWN, 1 + j].astype(F32) + slope_one[j] * joined(extra, j)
-
-    def gathered(f):
+
+    inners(grad_mid_slots, grad_mid, w_one, True)
+    for j in range(CAP):
+        low[j] = grad_mid[OWN, 1 + j].astype(F32) + slope_one[j] * slot(j)
+    for f in range(WINDOW):
         summed = mix[0, f] * low[0]
         for j in range(1, CAP):
             summed += mix[j, f] * low[j]
-        return summed
+        partial[f] = summed
+    start, stop = borders(grad_mid_edges, grad_mid_edge, w_one, True)
+    start = slope_one[0] * start
+    stop = slope_one[end] * stop
+
+    def gathered(f):
+        return partial[f] + mix[0, f] * start + mix[end, f] * stop
 
     spread_copies = []
-    for start, count, at, by in ((0, 2, 8, -2), (14, 2, 10, 2), (2, 4, 0, -1), (10, 4, 4, 1)):
-        for f in range(start, start + count):
+    for head, count, at, by in ((0, 2, 8, -2), (14, 2, 10, 2), (2, 4, 0, -1), (10, 4, 4, 1)):
+        for f in range(head, head + count):
             spread[f] = gathered(f).astype(BF16)
-        spread_copies.append(push(spread.at[pl.ds(start, count)], arrived.at[pl.ds(at, count)], by, r))
+        spread_copies.append(push(spread.at[pl.ds(head, count)], arrived.at[pl.ds(at, count)], by, r))
     for f in range(FRAMES):
         source_grad[f] = gathered(BELOW + f)
 
-    extra = convolve(act_two_slots, act_two_edges, act_two, act_two_edge, w_two, False)
-    for j in range(CAP):
-        value = joined(extra, j) + first[j].astype(F32) + b_two[...]
+    inners(act_two_slots, act_two, w_two, False)
+    start, stop = borders(act_two_edges, act_two_edge, w_two, False)
+    for j in range(CAP):
+        value = patched(slot(j), j, start, stop) + first[j].astype(F32) + b_two[...]
         decoded[j] = jnp.where(used[j], value, 0.0).astype(BF16)
 
     landed(*spread_copies)
@@ -434,7 +456,9 @@
                 wide_slots,
                 wide_slots,
                 pltpu.VMEM((3, CAP, W, C), F32),
-                pltpu.VMEM((3, W, C), F32),
+                pltpu.VMEM((2, 3, W, C), F32),
+                wide_slots,
+                pltpu.VMEM((WINDOW, W, C), F32),
                 box,
                 box,
                 box,

time: 30.1 us -> 30.5 us (1.013)
  Pallas kernels: 28.7 us -> 29.1 us
    pallas_call x1, Pallas kernels: 28 us -> 28.4 us  [body(): pl.pallas_call(lambda *refs: kernel(spans, lines, *refs), out_shape=(pltp...]
where the time goes in v6:
time: 30.5 us; the launch traced here: 30.4 us
  Pallas kernels  29.1 us (95%)
  between operations  1.29 us (4%)
    pallas_call x1, Pallas kernels, body(): pl.pallas_call(lambda *refs: kernel(spans, lines, *refs), out_shape=(pltp...  28.4 us
    pallas_call x1, Pallas kernels, body(): pl.pallas_call(finish, out_shape=(jax.ShapeDtypeStruct((CAP, W, C), BF16)...  0.72 us

profile of v6, /device:TPU:122, one launch (start us, length us, event | category | flops | bytes accessed | tf_op | source)
XLA Modules:
  0.0 30.4 jit_solution(13540798657899634893)
XLA Ops:
  1.3 28.4 %shard_map.104 = (bf16[9,32,256]{2,1,0:T(8,128)(2,1)S(1)}, f32[4,32,256]{2,1,0:T(8,128)S(1)}) custom-call(bf16[4,32,256]{2,1,0:T(8,128)(2,1)} %bitcast.15, s32[1]{0:T(128)S(6)} %copy.13.refs_1_, s32[4,9]{1,0:T(4,128)} %bitcast.16, f32[4,9]{1,0:T(4,128)} %bitcast.17, bf16[3,3,3,256,256]{4,3,2,1,0:T(8,128)(2,1)} %refs_4_.1, f32[1,256]{1,0:T(1,128)} %bitcast.18, ...), custom_call_target="tpu_custom_call" | custom-call | flops 4076863488 | bytes 7077888 | tf_op jit(solution)/shard_map/pallas_call | solution.py:438
  29.6 0.7 %shard_map.105 = (bf16[9,32,256]{2,1,0:T(8,128)(2,1)}, f32[4,32,256]{2,1,0:T(8,128)}) custom-call(bf16[9,32,256]{2,1,0:T(8,128)(2,1)S(1)} %get-tuple-element.6.decoded_in, f32[4,32,256]{2,1,0:T(8,128)S(1)} %get-tuple-element.7.grad_in), custom_call_target="tpu_custom_call" | custom-call | tf_op jit(solution)/shard_map/pallas_call | solution.py:505

commit v7 on v6

--- a/solution.py
+++ b/solution.py
@@ -14,6 +14,7 @@
 W = 32
 C = 256
 OWN, NEAR, FAR = 0, 1, 2
+ENDS = {3: (0, 4), 6: (4, 7), 8: (7, 9)}
 BF16 = jnp.bfloat16
 F32 = jnp.float32
 
@@ -164,11 +165,13 @@
         near_edges = push(ends, edge.at[0, NEAR], 1, near), push(head, edge.at[1, NEAR], -1, near)
         return own_edges, near_edges, far_edges
 
-    def send_slots(box):
-        mine = box.at[OWN, pl.ds(1, CAP)]
-        far_mine = push(mine, box.at[FAR, pl.ds(1, CAP)], 0, far)
-        near_mine = push(mine, box.at[NEAR, pl.ds(1, CAP)], 0, near)
-        return None, near_mine, far_mine
+    def send_far(box, low_slot, high_slot):
+        span = pl.ds(1 + low_slot, high_slot - low_slot)
+        return push(box.at[OWN, span], box.at[FAR, span], 0, far)
+
+    def send_near(box):
+        span = pl.ds(1, CAP)
+        return push(box.at[OWN, span], box.at[NEAR, span], 0, near)
 
     get_source.wait()
     pl.semaphore_wait(barrier, greeted)
@@ -195,7 +198,7 @@
 
     end = jnp.clip(filled - 1, 0, CAP - 1)
     last[0] = raw[end]
-    inc_slots = send_slots(inc)
+    inc_slots = (None, [send_near(inc)], [send_far(inc, 0, CAP)])
     edges = (
         push(last.at[0], inc_edge.at[0, OWN], 1, r),
         push(inc.at[OWN, 1], inc_edge.at[1, OWN], -1, r),
@@ -215,21 +218,30 @@
 
     def inner(slots, box, w, back, s):
         def step():
-            if s != OWN:
-                slots[s][0].wait_recv()
-            fields = jnp.concatenate(
-                [box[s, a : a + CAP].reshape(CAP * W, C) for a in range(3)], axis=1
-            )
-            for c in range(3):
-                term = products(fields, w, s, back, c, (0, 1, 2))
-                if s == OWN:
-                    parts[c] = term.reshape(CAP, W, C)
-                else:
-                    parts[c] += term.reshape(CAP, W, C)
+            pieces = 1 if s == OWN else len(slots[s])
+            for k in range(pieces):
+                if s != OWN:
+                    slots[s][k][0].wait_recv()
+                low_slot, high_slot = (0, CAP) if pieces == 1 else (3 * k, 3 * k + 3)
+                held = high_slot - low_slot
+                fields = jnp.concatenate(
+                    [
+                        box[s, low_slot + a : high_slot + a].reshape(held * W, C)
+                        for a in range(3)
+                    ],
+                    axis=1,
+                )
+                for c in range(3):
+                    term = products(fields, w, s, back, c, (0, 1, 2)).reshape(held, W, C)
+                    if s == OWN:
+                        parts[c] = term
+                    else:
+                        parts[c, low_slot:high_slot] += term
 
         when(far_there if s == FAR else None, step)
         if s != OWN:
-            slots[s][4] = False
+            for entry in slots[s]:
+                entry[4] = False
 
     def border(edges, edge, w, back, s):
         landed(*edges[s])
@@ -309,11 +321,14 @@
     act_one[OWN, 1] = silu(value)
     last[1] = silu(blend(end))
     act_one_edges = send_edges(act_one, act_one_edge, last.at[1])
+    act_one_far = []
     for j in range(1, CAP):
         value = jnp.where(used[j], blend(j), none)
         blended[j] = value
         act_one[OWN, 1 + j] = silu(value)
-    act_one_slots = send_slots(act_one)
+        if j in ENDS:
+            act_one_far.append(send_far(act_one, *ENDS[j]))
+    act_one_slots = (None, [send_near(act_one)], act_one_far)
 
     start, stop = borders(inc_edges, inc_edge, w_two, True)
     for j in range(CAP):
@@ -350,10 +365,13 @@
     stop_grad = grad_at(end, stop_first)
     last[2] = stop_grad
     grad_mid_edges = send_edges(grad_mid, grad_mid_edge, last.at[2])
+    grad_mid_far = []
     for j in range(1, CAP):
         at_end = filled == j + 1
         grad_mid[OWN, 1 + j] = jnp.where(at_end, stop_grad, grad_mid[OWN, 1 + j])
-    grad_mid_slots = send_slots(grad_mid)
+        if j in ENDS:
+            grad_mid_far.append(send_far(grad_mid, *ENDS[j]))
+    grad_mid_slots = (None, [send_near(grad_mid)], grad_mid_far)
     act_two[OWN, 1] = silu(value)
     stop_act = silu(stop_first)
     last[3] = stop_act
@@ -362,7 +380,7 @@
         first[j] = jnp.where(at_end, stop_first, first[j])
         act_two[OWN, 1 + j] = jnp.where(at_end, stop_act, act_two[OWN, 1 + j])
     act_two_edges = send_edges(act_two, act_two_edge, last.at[3])
-    act_two_slots = send_slots(act_two)
+    act_two_slots = (None, [send_near(act_two)], [send_far(act_two, 0, CAP)])
 
     inners(grad_mid_slots, grad_mid, w_one, True)
     for j in range(CAP):
@@ -475,8 +493,8 @@
                 pltpu.SMEM((TAPS, CAP), jnp.int32),
                 pltpu.SMEM((TAPS, CAP), F32),
                 pltpu.SemaphoreType.DMA((9,)),
-                pltpu.SemaphoreType.DMA((40,)),
-                pltpu.SemaphoreType.DMA((40,)),
+                pltpu.SemaphoreType.DMA((44,)),
+                pltpu.SemaphoreType.DMA((44,)),
             ],
             compiler_params=pltpu.CompilerParams(
                 collective_id=0, has_side_effects=True, vmem_limit_bytes=48 * 1024 * 1024

time: 30.5 us -> 30.8 us (level)
    pallas_call x1, Pallas kernels: 28.4 us -> 28.7 us  [body(): pl.pallas_call(lambda *refs: kernel(spans, lines, *refs), out_shape=(pltp...]
where the time goes in v7:
time: 30.8 us; the launch traced here: 30.7 us
  Pallas kernels  29.4 us (95%)
  between operations  1.29 us (4%)
    pallas_call x1, Pallas kernels, body(): pl.pallas_call(lambda *refs: kernel(spans, lines, *refs), out_shape=(pltp...  28.7 us
    pallas_call x1, Pallas kernels, body(): pl.pallas_call(finish, out_shape=(jax.ShapeDtypeStruct((CAP, W, C), BF16)...  0.72 us

profile of v7, /device:TPU:122, one launch (start us, length us, event | category | flops | bytes accessed | tf_op | source)
XLA Modules:
  0.0 30.7 jit_solution(4560303346575881670)
XLA Ops:
  1.3 28.7 %shard_map.104 = (bf16[9,32,256]{2,1,0:T(8,128)(2,1)S(1)}, f32[4,32,256]{2,1,0:T(8,128)S(1)}) custom-call(bf16[4,32,256]{2,1,0:T(8,128)(2,1)} %bitcast.15, s32[1]{0:T(128)S(6)} %copy.13.refs_1_, s32[4,9]{1,0:T(4,128)} %bitcast.16, f32[4,9]{1,0:T(4,128)} %bitcast.17, bf16[3,3,3,256,256]{4,3,2,1,0:T(8,128)(2,1)} %refs_4_.1, f32[1,256]{1,0:T(1,128)} %bitcast.18, ...), custom_call_target="tpu_custom_call" | custom-call | flops 4076863488 | bytes 7077888 | tf_op jit(solution)/shard_map/pallas_call | solution.py:456
  30.0 0.7 %shard_map.105 = (bf16[9,32,256]{2,1,0:T(8,128)(2,1)}, f32[4,32,256]{2,1,0:T(8,128)}) custom-call(bf16[9,32,256]{2,1,0:T(8,128)(2,1)S(1)} %get-tuple-element.6.decoded_in, f32[4,32,256]{2,1,0:T(8,128)S(1)} %get-tuple-element.7.grad_in), custom_call_target="tpu_custom_call" | custom-call | tf_op jit(solution)/shard_map/pallas_call | solution.py:523

commit v8 on v6

--- a/solution.py
+++ b/solution.py
@@ -45,8 +45,6 @@
     slope_one,
     parts,
     fringe,
-    plain,
-    partial,
     inc,
     act_one,
     grad_mid,
@@ -280,14 +278,6 @@
     get_two.wait()
     inner(inc_slots, inc, w_two, True, OWN)
     inner(inc_slots, inc, w_two, True, NEAR)
-    landed(*edges)
-    for s, row in ((NEAR, near), (FAR, far)):
-        inc_edges.append(
-            [
-                push(inc_edge.at[k, OWN], inc_edge.at[k, s], 0, row, exists((-1, 1)[k]))
-                for k in range(2)
-            ]
-        )
     inner(inc_slots, inc, w_two, True, FAR)
     for j in range(CAP):
         back_two[j] = slot(j)
@@ -315,9 +305,14 @@
         act_one[OWN, 1 + j] = silu(value)
     act_one_slots = send_slots(act_one)
 
-    start, stop = borders(inc_edges, inc_edge, w_two, True)
-    for j in range(CAP):
-        back_two[j] = patched(back_two[j], j, start, stop)
+    landed(*edges)
+    for s, row in ((NEAR, near), (FAR, far)):
+        inc_edges.append(
+            [
+                push(inc_edge.at[k, OWN], inc_edge.at[k, s], 0, row, exists((-1, 1)[k]))
+                for k in range(2)
+            ]
+        )
 
     def slope(value):
         wide = value.astype(F32)
@@ -333,51 +328,46 @@
     get_one.wait()
     get_b_one.wait()
     get_b_two.wait()
-    inners(act_one_slots, act_one, w_one, False)
-    for j in range(CAP):
-        value = slot(j) + blended[j].astype(F32) + b_one[...]
-        plain[j] = value
-        if j > 0:
-            value = jnp.where(used[j], value.astype(BF16), none)
-            first[j] = value
-            grad_mid[OWN, 1 + j] = jnp.where(used[j], grad_at(j, value), none)
-            act_two[OWN, 1 + j] = silu(value)
+    inner(act_one_slots, act_one, w_one, False, OWN)
+    inner(act_one_slots, act_one, w_one, False, NEAR)
+    start, stop = borders(inc_edges, inc_edge, w_two, True)
+    for j in range(CAP):
+        back_two[j] = patched(back_two[j], j, start, stop)
+    inner(act_one_slots, act_one, w_one, False, FAR)
     start, stop = borders(act_one_edges, act_one_edge, w_one, False)
-    value = patched(plain[0], 0, start, stop).astype(BF16)
+
+    def first_at(j, conv):
+        return (conv + blended[j].astype(F32) + b_one[...]).astype(BF16)
+
+    value = first_at(0, patched(slot(0), 0, start, stop))
     first[0] = value
     grad_mid[OWN, 1] = grad_at(0, value)
-    stop_first = (plain[end] + stop + jnp.where(end == 0, start, 0.0)).astype(BF16)
-    stop_grad = grad_at(end, stop_first)
-    last[2] = stop_grad
+    value = first_at(end, slot(end) + stop + jnp.where(end == 0, start, 0.0))
+    last[2] = grad_at(end, value)
     grad_mid_edges = send_edges(grad_mid, grad_mid_edge, last.at[2])
+    last[3] = silu(value)
     for j in range(1, CAP):
-        at_end = filled == j + 1
-        grad_mid[OWN, 1 + j] = jnp.where(at_end, stop_grad, grad_mid[OWN, 1 + j])
+        value = first_at(j, patched(slot(j), j, start, stop))
+        value = jnp.where(used[j], value, none)
+        first[j] = value
+        grad_mid[OWN, 1 + j] = jnp.where(used[j], grad_at(j, value), none)
     grad_mid_slots = send_slots(grad_mid)
-    act_two[OWN, 1] = silu(value)
-    stop_act = silu(stop_first)
-    last[3] = stop_act
-    for j in range(1, CAP):
-        at_end = filled == j + 1
-        first[j] = jnp.where(at_end, stop_first, first[j])
-        act_two[OWN, 1 + j] = jnp.where(at_end, stop_act, act_two[OWN, 1 + j])
+    for j in range(CAP):
+        act_two[OWN, 1 + j] = silu(first[j])
     act_two_edges = send_edges(act_two, act_two_edge, last.at[3])
     act_two_slots = send_slots(act_two)
 
     inners(grad_mid_slots, grad_mid, w_one, True)
-    for j in range(CAP):
-        low[j] = grad_mid[OWN, 1 + j].astype(F32) + slope_one[j] * slot(j)
-    for f in range(WINDOW):
+    start, stop = borders(grad_mid_edges, grad_mid_edge, w_one, True)
+    for j in range(CAP):
+        value = patched(slot(j), j, start, stop)
+        low[j] = grad_mid[OWN, 1 + j].astype(F32) + slope_one[j] * value
+
+    def gathered(f):
         summed = mix[0, f] * low[0]
         for j in range(1, CAP):
             summed += mix[j, f] * low[j]
-        partial[f] = summed
-    start, stop = borders(grad_mid_edges, grad_mid_edge, w_one, True)
-    start = slope_one[0] * start
-    stop = slope_one[end] * stop
-
-    def gathered(f):
-        return partial[f] + mix[0, f] * start + mix[end, f] * stop
+        return summed
 
     spread_copies = []
     for head, count, at, by in ((0, 2, 8, -2), (14, 2, 10, 2), (2, 4, 0, -1), (10, 4, 4, 1)):
@@ -457,8 +447,6 @@
                 wide_slots,
                 pltpu.VMEM((3, CAP, W, C), F32),
                 pltpu.VMEM((2, 3, W, C), F32),
-                wide_slots,
-                pltpu.VMEM((WINDOW, W, C), F32),
                 box,
                 box,
                 box,

time: 30.5 us -> 29.9 us (0.980); the launches traced: 30.4 us -> 29.4 us
  Pallas kernels: 29.1 us -> 28.1 us
    pallas_call x1, Pallas kernels: 28.4 us -> 27.3 us  [body(): pl.pallas_call(lambda *refs: kernel(spans, lines, *refs), out_shape=(pltp...]
where the time goes in v8:
time: 29.9 us; the launch traced here: 29.4 us
  Pallas kernels  28.1 us (94%)
  between operations  1.29 us (4%)
    pallas_call x1, Pallas kernels, body(): pl.pallas_call(lambda *refs: kernel(spans, lines, *refs), out_shape=(pltp...  27.3 us
    pallas_call x1, Pallas kernels, body(): pl.pallas_call(finish, out_shape=(jax.ShapeDtypeStruct((CAP, W, C), BF16)...  0.72 us

profile of v8, /device:TPU:122, one launch (start us, length us, event | category | flops | bytes accessed | tf_op | source)
XLA Modules:
  0.0 29.4 jit_solution(5131148664385047304)
XLA Ops:
  1.3 27.3 %shard_map.104 = (bf16[9,32,256]{2,1,0:T(8,128)(2,1)S(1)}, f32[4,32,256]{2,1,0:T(8,128)S(1)}) custom-call(bf16[4,32,256]{2,1,0:T(8,128)(2,1)} %bitcast.15, s32[1]{0:T(128)S(6)} %copy.13.refs_1_, s32[4,9]{1,0:T(4,128)} %bitcast.16, f32[4,9]{1,0:T(4,128)} %bitcast.17, bf16[3,3,3,256,256]{4,3,2,1,0:T(8,128)(2,1)} %refs_4_.1, f32[1,256]{1,0:T(1,128)} %bitcast.18, ...), custom_call_target="tpu_custom_call" | custom-call | flops 4076863488 | bytes 7077888 | tf_op jit(solution)/shard_map/pallas_call | solution.py:428
  28.6 0.7 %shard_map.105 = (bf16[9,32,256]{2,1,0:T(8,128)(2,1)}, f32[4,32,256]{2,1,0:T(8,128)}) custom-call(bf16[9,32,256]{2,1,0:T(8,128)(2,1)S(1)} %get-tuple-element.6.decoded_in, f32[4,32,256]{2,1,0:T(8,128)S(1)} %get-tuple-element.7.grad_in), custom_call_target="tpu_custom_call" | custom-call | tf_op jit(solution)/shard_map/pallas_call | solution.py:493

commit v9 on v8

--- a/solution.py
+++ b/solution.py
@@ -45,6 +45,7 @@
     slope_one,
     parts,
     fringe,
+    partial,
     inc,
     act_one,
     grad_mid,
@@ -127,7 +128,7 @@
 
     copies = []
 
-    def push(src, dst, by, row, held=None):
+    def push(src, dst, by, row, held=None, now=True):
         k = len(copies)
         copy = pltpu.make_async_remote_copy(
             src_ref=src,
@@ -138,7 +139,8 @@
             device_id_type=MESH,
         )
         sent = both(both(exists(by), line(row)), held)
-        when(sent, copy.start)
+        if now:
+            when(sent, copy.start)
         entry = [copy, sent, both(both(exists(-by), line(row)), held), True, True]
         copies.append(entry)
         return entry
@@ -156,11 +158,21 @@
                 entry[3] = False
 
     def send_edges(box, edge, ends):
-        head = box.at[OWN, 1]
-        far_edges = push(ends, edge.at[0, FAR], 1, far), push(head, edge.at[1, FAR], -1, far)
-        own_edges = push(ends, edge.at[0, OWN], 1, r), push(head, edge.at[1, OWN], -1, r)
-        near_edges = push(ends, edge.at[0, NEAR], 1, near), push(head, edge.at[1, NEAR], -1, near)
-        return own_edges, near_edges, far_edges
+        edges = [None] * 3
+        for s, row in ((FAR, far), (OWN, r), (NEAR, near)):
+            edges[s] = (
+                push(ends, edge.at[0, s], 1, row, now=False),
+                push(box.at[OWN, 1], edge.at[1, s], -1, row, now=False),
+            )
+        for side, by in ((0, 1), (1, -1)):
+
+            def start(side=side):
+                when(far_there, edges[FAR][side][0].start)
+                edges[OWN][side][0].start()
+                edges[NEAR][side][0].start()
+
+            when(exists(by), start)
+        return edges
 
     def send_slots(box):
         mine = box.at[OWN, pl.ds(1, CAP)]
@@ -358,16 +370,19 @@
     act_two_slots = send_slots(act_two)
 
     inners(grad_mid_slots, grad_mid, w_one, True)
-    start, stop = borders(grad_mid_edges, grad_mid_edge, w_one, True)
-    for j in range(CAP):
-        value = patched(slot(j), j, start, stop)
-        low[j] = grad_mid[OWN, 1 + j].astype(F32) + slope_one[j] * value
-
-    def gathered(f):
+    for j in range(CAP):
+        low[j] = grad_mid[OWN, 1 + j].astype(F32) + slope_one[j] * slot(j)
+    for f in range(WINDOW):
         summed = mix[0, f] * low[0]
         for j in range(1, CAP):
             summed += mix[j, f] * low[j]
-        return summed
+        partial[f] = summed
+    start, stop = borders(grad_mid_edges, grad_mid_edge, w_one, True)
+    start = slope_one[0] * start
+    stop = slope_one[end] * stop
+
+    def gathered(f):
+        return partial[f] + mix[0, f] * start + mix[end, f] * stop
 
     spread_copies = []
     for head, count, at, by in ((0, 2, 8, -2), (14, 2, 10, 2), (2, 4, 0, -1), (10, 4, 4, 1)):
@@ -382,7 +397,7 @@
     for j in range(CAP):
         value = patched(slot(j), j, start, stop) + first[j].astype(F32) + b_two[...]
         decoded[j] = jnp.where(used[j], value, 0.0).astype(BF16)
-
+    left(*copies)
     landed(*spread_copies)
     for f in range(FRAMES):
         value = source_grad[f]
@@ -393,7 +408,6 @@
         else:
             value += jnp.where(exists(-2), arrived[10 + f].astype(F32), 0.0)
         source_grad[f] = value
-    left(*copies)
 
 
 def finish(decoded_in, grad_in, decoded, source_grad, done):
@@ -447,6 +461,7 @@
                 wide_slots,
                 pltpu.VMEM((3, CAP, W, C), F32),
                 pltpu.VMEM((2, 3, W, C), F32),
+                pltpu.VMEM((WINDOW, W, C), F32),
                 box,
                 box,
                 box,

time: 29.9 us -> 29.7 us (level); the launches traced: 29.4 us -> 29.6 us
  no operation moved by 1% of the time
where the time goes in v9:
time: 29.7 us; the launch traced here: 29.6 us
  Pallas kernels  28.3 us (95%)
  between operations  1.29 us (4%)
    pallas_call x1, Pallas kernels, body(): pl.pallas_call(lambda *refs: kernel(spans, lines, *refs), out_shape=(pltp...  27.6 us
    pallas_call x1, Pallas kernels, body(): pl.pallas_call(finish, out_shape=(jax.ShapeDtypeStruct((CAP, W, C), BF16)...  0.72 us

profile of v9, /device:TPU:122, one launch (start us, length us, event | category | flops | bytes accessed | tf_op | source)
XLA Modules:
  0.0 29.6 jit_solution(14385577782292953107)
XLA Ops:
  1.3 27.6 %shard_map.104 = (bf16[9,32,256]{2,1,0:T(8,128)(2,1)S(1)}, f32[4,32,256]{2,1,0:T(8,128)S(1)}) custom-call(bf16[4,32,256]{2,1,0:T(8,128)(2,1)} %bitcast.15, s32[1]{0:T(128)S(6)} %copy.13.refs_1_, s32[4,9]{1,0:T(4,128)} %bitcast.16, f32[4,9]{1,0:T(4,128)} %bitcast.17, bf16[3,3,3,256,256]{4,3,2,1,0:T(8,128)(2,1)} %refs_4_.1, f32[1,256]{1,0:T(1,128)} %bitcast.18, ...), custom_call_target="tpu_custom_call" | custom-call | flops 4076863488 | bytes 7077888 | tf_op jit(solution)/shard_map/pallas_call | solution.py:442
  28.9 0.7 %shard_map.105 = (bf16[9,32,256]{2,1,0:T(8,128)(2,1)}, f32[4,32,256]{2,1,0:T(8,128)}) custom-call(bf16[9,32,256]{2,1,0:T(8,128)(2,1)S(1)} %get-tuple-element.6.decoded_in, f32[4,32,256]{2,1,0:T(8,128)S(1)} %get-tuple-element.7.grad_in), custom_call_target="tpu_custom_call" | custom-call | tf_op jit(solution)/shard_map/pallas_call | solution.py:508

commit v10 on v9

--- a/solution.py
+++ b/solution.py
@@ -167,9 +167,9 @@
         for side, by in ((0, 1), (1, -1)):
 
             def start(side=side):
-                when(far_there, edges[FAR][side][0].start)
                 edges[OWN][side][0].start()
                 edges[NEAR][side][0].start()
+                when(far_there, edges[FAR][side][0].start)
 
             when(exists(by), start)
         return edges
@@ -311,12 +311,6 @@
     act_one[OWN, 1] = silu(value)
     last[1] = silu(blend(end))
     act_one_edges = send_edges(act_one, act_one_edge, last.at[1])
-    for j in range(1, CAP):
-        value = jnp.where(used[j], blend(j), none)
-        blended[j] = value
-        act_one[OWN, 1 + j] = silu(value)
-    act_one_slots = send_slots(act_one)
-
     landed(*edges)
     for s, row in ((NEAR, near), (FAR, far)):
         inc_edges.append(
@@ -325,6 +319,11 @@
                 for k in range(2)
             ]
         )
+    for j in range(1, CAP):
+        value = jnp.where(used[j], blend(j), none)
+        blended[j] = value
+        act_one[OWN, 1 + j] = silu(value)
+    act_one_slots = send_slots(act_one)
 
     def slope(value):
         wide = value.astype(F32)

time: 29.7 us -> 29.5 us (level)
  Pallas kernels: 28.3 us -> 28 us
    pallas_call x1, Pallas kernels: 27.6 us -> 27.3 us  [body(): pl.pallas_call(lambda *refs: kernel(spans, lines, *refs), out_shape=(pltp...]
where the time goes in v10:
time: 29.5 us; the launch traced here: 29.3 us
  Pallas kernels  28 us (95%)
  between operations  1.29 us (4%)
    pallas_call x1, Pallas kernels, body(): pl.pallas_call(lambda *refs: kernel(spans, lines, *refs), out_shape=(pltp...  27.3 us
    pallas_call x1, Pallas kernels, body(): pl.pallas_call(finish, out_shape=(jax.ShapeDtypeStruct((CAP, W, C), BF16)...  0.72 us

profile of v10, /device:TPU:122, one launch (start us, length us, event | category | flops | bytes accessed | tf_op | source)
XLA Modules:
  0.0 29.3 jit_solution(12779477175693797019)
XLA Ops:
  1.3 27.3 %shard_map.104 = (bf16[9,32,256]{2,1,0:T(8,128)(2,1)S(1)}, f32[4,32,256]{2,1,0:T(8,128)S(1)}) custom-call(bf16[4,32,256]{2,1,0:T(8,128)(2,1)} %bitcast.15, s32[1]{0:T(128)S(6)} %copy.13.refs_1_, s32[4,9]{1,0:T(4,128)} %bitcast.16, f32[4,9]{1,0:T(4,128)} %bitcast.17, bf16[3,3,3,256,256]{4,3,2,1,0:T(8,128)(2,1)} %refs_4_.1, f32[1,256]{1,0:T(1,128)} %bitcast.18, ...), custom_call_target="tpu_custom_call" | custom-call | flops 4076863488 | bytes 7077888 | tf_op jit(solution)/shard_map/pallas_call | solution.py:441
  28.6 0.7 %shard_map.105 = (bf16[9,32,256]{2,1,0:T(8,128)(2,1)}, f32[4,32,256]{2,1,0:T(8,128)}) custom-call(bf16[9,32,256]{2,1,0:T(8,128)(2,1)S(1)} %get-tuple-element.6.decoded_in, f32[4,32,256]{2,1,0:T(8,128)S(1)} %get-tuple-element.7.grad_in), custom_call_target="tpu_custom_call" | custom-call | tf_op jit(solution)/shard_map/pallas_call | solution.py:507
